TPU v7x, 32 devices: a whole 2x2x4 slice. The times are simulated.
32 devices in a mesh: px: 4 (over x, core), py: 8 (over z, y).
Axes of the slice: x: 2, y: 2, z: 4, core: 2. Of those that a mesh axis runs over, the one named last changes fastest.
Arguments:
- theta_field: float32 [32, 64, 1024], P(None, 'px', 'py'), may hold values from -6 to 6
- wind_u: float32 [32, 64, 1024], P(None, 'px', 'py'), may hold values from -6 to 6
- wind_v: float32 [32, 64, 1024], P(None, 'px', 'py'), may hold values from -6 to 6
- hyper_coef: float32 [32], replicated, may hold values from 0.002 to 0.02
- damp_coef: float32 [32], replicated, may hold values from 0.05 to 0.4
- obs_cells: int32 [32, 32, 512], P(('px', 'py')), may hold values from 0 to 1918, as said below
- obs_levels: int32 [32, 32, 512], P(('px', 'py')), may hold values from 0 to 30
- obs_bary: float32 [32, 32, 3, 512], P(('px', 'py')), may hold values from 0 to 1, as said below
- obs_vfrac: float32 [32, 32, 512], P(('px', 'py')), may hold values from 0 to 1
- obs_values: float32 [32, 32, 512], P(('px', 'py')), may hold values from -6 to 6
- obs_mask: int32 [32, 32, 512], P(('px', 'py')), may hold values from 0 to 1, as said below
Outputs:
- theta_next: float32 [32, 64, 1024], P(None, 'px', 'py')
- wind_u_next: float32 [32, 64, 1024], P(None, 'px', 'py')
- wind_v_next: float32 [32, 64, 1024], P(None, 'px', 'py')
- departures: float32 [32, 32, 512], P(('px', 'py'))
Inputs may be any that keep to these rules, and one draw needn't show every extreme that they name: obs_cells is r * 128 + c with r below 15 and c below 127. `obs_bary`: each row of three weights is positive and sums to one. `obs_mask`: in every draw some destination patch has all 512 slots used from every owner.
All inputs are finite; a program needn't handle non-finite values.
Results may differ from a plain program's by a relative error of at most 0.000084.
Values sent between devices are 32-bit elements; how exact they have to be, the bound alone decides.
A program may use at most 64 MiB of HBM per device.

v0:
```python
import math

import jax
import jax.numpy as jnp
from jax import lax
from jax.sharding import PartitionSpec as P


def padded(cells, sides, width):
    for axis, dim in sides:
        count = lax.axis_size(axis)
        head = lax.slice_in_dim(cells, 0, width, axis=dim)
        tail = lax.slice_in_dim(cells, cells.shape[dim] - width, cells.shape[dim], axis=dim)
        cells = jnp.concatenate(
            [
                lax.ppermute(tail, axis, [(i, (i + 1) % count) for i in range(count)]),
                cells,
                lax.ppermute(head, axis, [((i + 1) % count, i) for i in range(count)]),
            ],
            axis=dim,
        )
    return cells


def inner_view(field, step_i, step_j):
    rows = field.shape[-2]
    cols = field.shape[-1]
    return field[..., 1 + step_i : rows - 1 + step_i, 1 + step_j : cols - 1 + step_j]


def laplace(field):
    total = inner_view(field, 1, 0) + inner_view(field, -1, 0)
    total = total + inner_view(field, 0, 1) + inner_view(field, 0, -1)
    total = total + inner_view(field, 1, -1) + inner_view(field, -1, 1)
    return total - 6.0 * inner_view(field, 0, 0)


def diff_x(field):
    return (inner_view(field, 1, 0) - inner_view(field, -1, 0)) * 0.5


def diff_y(field):
    return (inner_view(field, 0, 1) - inner_view(field, 0, -1)) * 0.5


def interpolate(theta_next, cells, levels, bary, vfrac):
    levs = theta_next.shape[0]
    cols = theta_next.shape[2]
    count = theta_next.shape[1] * cols
    per_cell = theta_next.reshape(levs, count).T
    table = jnp.concatenate(
        [per_cell, jnp.roll(per_cell, -cols, axis=0), jnp.roll(per_cell, -1, axis=0)], axis=1
    )
    shape = cells.shape
    total = cells.size
    block = math.gcd(total, 2048)
    flat_cells = cells.reshape(total // block, block)
    flat_levels = levels.reshape(total // block, block)
    flat_vfrac = vfrac.reshape(total // block, block)
    flat_bary = jnp.moveaxis(bary, -2, 0).reshape(3, total // block, block)
    flat_bary = jnp.moveaxis(flat_bary, 0, 1)
    cell_iota = jnp.arange(count, dtype=jnp.int32)
    level_iota = jnp.arange(levs, dtype=jnp.int32)

    def one_block(pieces):
        blk_cells, blk_levels, blk_vfrac, blk_bary = pieces
        onehot = (blk_cells[:, None] == cell_iota[None, :]).astype(jnp.float32)
        picked = jnp.dot(
            onehot, table, preferred_element_type=jnp.float32, precision=lax.Precision.HIGHEST
        )
        picked = picked.reshape(block, 3, levs)
        weights = (1.0 - blk_vfrac[:, None]) * (level_iota[None, :] == blk_levels[:, None]).astype(
            jnp.float32
        )
        weights = weights + blk_vfrac[:, None] * (
            level_iota[None, :] == blk_levels[:, None] + 1
        ).astype(jnp.float32)
        columns = jnp.sum(picked * weights[:, None, :], axis=2)
        return jnp.sum(columns * blk_bary.T, axis=1)

    model = lax.map(one_block, (flat_cells, flat_levels, flat_vfrac, flat_bary))
    return model.reshape(shape)


def on_device(
    theta_field,
    wind_u,
    wind_v,
    hyper_coef,
    damp_coef,
    obs_cells,
    obs_levels,
    obs_bary,
    obs_vfrac,
    obs_values,
    obs_mask,
):
    stacked = jnp.stack([wind_u, wind_v, theta_field])
    bordered = padded(stacked, (("px", 2), ("py", 3)), 1)
    first_lap = laplace(bordered)
    divergence = diff_x(bordered[0]) + diff_y(bordered[1])
    theta_dx = diff_x(bordered[2])
    theta_dy = diff_y(bordered[2])
    joined = jnp.concatenate([first_lap, divergence[None]], axis=0)
    second = padded(joined, (("px", 2), ("py", 3)), 1)
    second_lap = laplace(second[:3])
    grad_x = diff_x(second[3])
    grad_y = diff_y(second[3])
    coef = hyper_coef[:, None, None]
    damp = damp_coef[:, None, None]
    theta_next = theta_field - coef * second_lap[2] - 0.5 * (wind_u * theta_dx + wind_v * theta_dy)
    wind_u_next = wind_u - coef * second_lap[0] + damp * grad_x
    wind_v_next = wind_v - coef * second_lap[1] + damp * grad_y
    got_cells, got_levels, got_bary, got_vfrac = (
        lax.all_to_all(obs_cells, ("px", "py"), split_axis=1, concat_axis=0, tiled=True),
        lax.all_to_all(obs_levels, ("px", "py"), split_axis=1, concat_axis=0, tiled=True),
        lax.all_to_all(obs_bary, ("px", "py"), split_axis=1, concat_axis=0, tiled=True),
        lax.all_to_all(obs_vfrac, ("px", "py"), split_axis=1, concat_axis=0, tiled=True),
    )
    model_here = interpolate(theta_next, got_cells, got_levels, got_bary, got_vfrac)
    model = lax.all_to_all(model_here, ("px", "py"), split_axis=0, concat_axis=1, tiled=True)
    departures = obs_mask.astype(jnp.float32) * (obs_values - model)
    return (theta_next, wind_u_next, wind_v_next, departures)


def solution(mesh):
    in_specs = (
        P(None, "px", "py"),
        P(None, "px", "py"),
        P(None, "px", "py"),
        P(),
        P(),
        P(("px", "py"), None, None),
        P(("px", "py"), None, None),
        P(("px", "py"), None, None, None),
        P(("px", "py"), None, None),
        P(("px", "py"), None, None),
        P(("px", "py"), None, None),
    )
    out_specs = (
        P(None, "px", "py"),
        P(None, "px", "py"),
        P(None, "px", "py"),
        P(("px", "py"), None, None),
    )
    return jax.shard_map(
        on_device, mesh=mesh, in_specs=in_specs, out_specs=out_specs, check_vma=False
    )
```

profile of v0, /device:TPU:0, one launch (start us, length us, event | category | flops | bytes accessed | tf_op | source)
XLA Modules:
  0.0 220.5 jit_solution(10910583006157783786)
XLA Ops:
  0.6 2.0 pad_maximum_fusion.15
  2.7 2.0 copy.165
  4.7 2.4 %collective-permute-start = (f32[3,32,1,128]{1,3,2,0:T(8,128)S(1)}, f32[3,32,1,128]{1,3,2,0:T(8,128)S(1)}, u32[]{:S(2)}, u32[]{:S(2)}) collective-permute-start(f32[3,32,1,128]{1,3,2,0:T(8,128)S(1)} %get-tuple-element.189), channel_id=1, source_target_pairs={{8,0},{16,8},{24,16},{0,24},{9,1},{17,9},{25,17},{1,25},{10,2},{18... | collective-permute-start | bytes 147464 | tf_op jit(solution)/shard_map/ppermute | solution.py:18
  7.1 5.2 %collective-permute-done = f32[3,32,1,128]{1,3,2,0:T(8,128)S(1)} collective-permute-done((f32[3,32,1,128]{1,3,2,0:T(8,128)S(1)}, f32[3,32,1,128]{1,3,2,0:T(8,128)S(1)}, u32[]{:S(2)}, u32[]{:S(2)}) %collective-permute-start) | collective-permute-done | bytes 49184 | tf_op jit(solution)/shard_map/ppermute | solution.py:18
  12.4 1.1 collective-permute-done.1
  14.1 4.6 %collective-permute-start.2 = (f32[3,32,18,1]{1,3,2,0:T(1,128)}, f32[3,32,18,1]{1,3,2,0:T(1,128)}, u32[]{:S(2)}, u32[]{:S(2)}) collective-permute-start(f32[3,32,18,1]{1,3,2,0:T(1,128)} %get-tuple-element.187), channel_id=1, source_target_pairs={{1,0},{2,1},{3,2},{4,3},{5,4},{6,5},{7,6},{0,7},{9,8},{10,9},{11,1... | collective-permute-start | bytes 20744 | tf_op jit(solution)/shard_map/ppermute | solution.py:18
  19.4 6.1 %all-to-all-start = ((s32[1,32,512]{2,0,1:T(1,128)}), s32[1,32,512]{2,0,1:T(1,128)}, u32[]{:S(2)}, u32[]{:S(2)}) async-start(s32[1,32,512]{2,0,1:T(1,128)} %copy.182), calls=%async_computation | async-start | bytes 131072 | tf_op jit(solution)/shard_map/all_to_all | solution.py:115
  25.6 1.3 pad_maximum_fusion.2
  26.8 1.3 slice_bitcast_fusion.2
  28.5 2.7 %maximum_maximum_fusion.1 = (f32[3,32,18,129]{1,3,2,0:T(8,128)S(1)}, f32[3,32,18,129]{1,3,2,0:T(8,128)S(1)}) fusion(f32[3,32,1,128]{1,3,2,0:T(8,128)S(1)} %collective-permute-done, f32[3,32,16,128]{1,3,2,0:T(8,128)S(1)} %copy.165, f32[3,32,1,128]{1,3,2,0:T(8,128)S(1)} %collective-permute-done.1, f32[3,32,18,1]{1,3,2,0:T(1,128)} %collective-permute-done.3, ...), kind=kLoop, calls=%fused_computation.21 | loop fusion | flops 1337472 | bytes 2681856 | tf_op jit(solution)/shard_map/concatenate | solution.py:14
  31.2 5.1 %fusion.10 = f32[3,32,16,128]{1,3,2,0:T(8,128)S(1)} fusion(f32[3,32,18,129]{1,3,2,0:T(8,128)S(1)} %get-tuple-element.185, f32[3,32,18,129]{1,3,2,0:T(8,128)S(1)} %get-tuple-element.184, f32[3,32,16,128]{1,3,2,0:T(8,128)} %copy-done, f32[3,32,1,128]{1,3,2,0:T(8,128)S(1)} %collective-permute-done.1, f32[3,32,1,128]{1,3,2,0:T(8,128)S(1)} %collective-permute-done), kind=kLoop, calls=%fused_computation.34 | loop fusion | flops 1769472 | bytes 4816896 | tf_op jit(solution)/shard_map/sub | solution.py:35
  37.2 1.4 collective-permute-start.4
  39.3 5.8 %all-to-all-start.1 = ((s32[1,32,512]{2,0,1:T(1,128)}), s32[1,32,512]{2,0,1:T(1,128)S(1)}, u32[]{:S(2)}, u32[]{:S(2)}) async-start(s32[1,32,512]{2,0,1:T(1,128)} %copy.184), calls=%async_computation.1 | async-start | bytes 131072 | tf_op jit(solution)/shard_map/all_to_all | solution.py:116
  46.4 1.0 pad_maximum_fusion.18
  48.0 4.5 %collective-permute-start.6 = (f32[4,32,18,1]{1,0,3,2:T(4,128)}, f32[4,32,18,1]{1,0,3,2:T(4,128)}, u32[]{:S(2)}, u32[]{:S(2)}) collective-permute-start(f32[4,32,18,1]{1,0,3,2:T(4,128)} %copy.170), channel_id=1, source_target_pairs={{1,0},{2,1},{3,2},{4,3},{5,4},{6,5},{7,6},{0,7},{9,8},{10,9},{11,1... | collective-permute-start | bytes 27656 | tf_op jit(solution)/shard_map/ppermute | solution.py:18
  53.1 5.9 %all-to-all-start.2 = ((f32[1,32,512]{2,0,1:T(1,128)}), f32[1,32,512]{2,0,1:T(1,128)S(1)}, u32[]{:S(2)}, u32[]{:S(2)}) async-start(f32[1,32,512]{2,0,1:T(1,128)} %copy.185), calls=%async_computation.2 | async-start | bytes 131072 | tf_op jit(solution)/shard_map/all_to_all | solution.py:118
  59.1 2.3 %copy.174 = f32[32,16,128]{0,2,1:T(8,128)} copy(f32[32,16,128]{2,1,0:T(8,128)} %param.13) | data formatting | bytes 524288 | tf_op args[0]
  61.3 2.2 %copy.175 = f32[32,16,128]{0,2,1:T(8,128)} copy(f32[32,16,128]{2,1,0:T(8,128)} %param.14) | data formatting | bytes 524288 | tf_op args[1]
  63.6 2.3 %copy.176 = f32[32,16,128]{0,2,1:T(8,128)} copy(f32[32,16,128]{2,1,0:T(8,128)} %param.15) | data formatting | bytes 524288 | tf_op args[2]
  65.9 1.8 copy.186
  67.7 1.6 reduce
  69.3 1.5 reshape.143
  71.6 1.5 reshape.145
  73.1 6.1 %all-to-all-start.3 = ((f32[1,32,3,512]{3,2,0,1:T(4,128)}), f32[1,32,3,512]{3,2,0,1:T(4,128)}, u32[]{:S(2)}, u32[]{:S(2)}) async-start(f32[1,32,3,512]{3,2,0,1:T(4,128)} %copy.186), calls=%async_computation.3 | async-start | bytes 524288 | tf_op jit(solution)/shard_map/all_to_all | solution.py:117
  81.7 4.5 %maximum_maximum_fusion = (f32[4,32,18,129]{1,3,2,0:T(8,128)S(1)}, f32[4,32,18,129]{1,3,2,0:T(8,128)S(1)}) fusion(f32[4,32,1,128]{1,3,2,0:T(8,128)S(1)} %collective-permute-done.4, f32[1,32,16,128]{1,3,2,0:T(8,128)} %copy-done.1, f32[3,32,16,128]{1,3,2,0:T(8,128)S(1)} %fusion.10, f32[4,32,1,128]{1,3,2,0:T(8,128)} %collective-permute-done.5, ...), kind=kLoop, calls=%fused_computation.19 | loop fusion | flops 2377728 | bytes 3575808 | tf_op jit(solution)/shard_map/concatenate | solution.py:14
  86.2 1.0 fusion.12
  87.2 3.3 %fusion.8 = f32[3,32,16,128]{1,3,2,0:T(8,128)S(1)} fusion(f32[4,32,18,129]{1,3,2,0:T(8,128)S(1)} %get-tuple-element.173, f32[4,32,18,129]{1,3,2,0:T(8,128)S(1)} %get-tuple-element.172, f32[4,32,1,128]{1,3,2,0:T(8,128)} %collective-permute-done.5, f32[1,32,16,128]{1,3,2,0:T(8,128)S(1)} %copy-done.2, f32[3,32,16,128]{1,3,2,0:T(8,128)S(1)} %fusion.10, ...), kind=kLoop, calls=%fused_computation.24 | loop fusion | flops 2162688 | bytes 5111808 | tf_op jit(solution)/shard_map/sub | solution.py:35
  90.6 1.2 fusion.14
  92.2 1.0 fusion.33
  93.2 2.5 %copy.188 = f32[2048,96]{1,0:T(8,128)} copy(f32[2048,96]{0,1:T(8,128)} %fusion.33) | data formatting | bytes 1572864
  95.7 1.0 copy.187
  96.8 108.5 %while.12 = (s32[]{:T(128)}, f32[8,2048]{1,0:T(8,128)}, s32[8,2048]{1,0:T(8,128)}, f32[2048,96]{1,0:T(8,128)}, s32[8,2048]{1,0:T(8,128)}, /*index=5*/f32[8,2048]...) while((s32[]{:T(128)}, f32[8,2048]{1,0:T(8,128)}, s32[8,2048]{1,0:T(8,128)}, ...), condition=%wide.region_3.4_spmd.clone.clone, body=%wide.region_0.3_spmd.clone.clone.sunk | while | flops 4836761600 | bytes 3154029 | solution.py:81
  96.8 0.9 constant_dynamic-slice_fusion.7
  98.6 10.0 %fusion.41 = f32[2048,96]{0,1:T(8,128)S(1)} fusion(f32[2048,96]{1,0:T(8,128)} %get-tuple-element.258, s32[2048]{0:T(1024)S(1)} %bitcast.95), kind=kOutput, calls=%fused_computation.3.clone.1 | convolution fusion | flops 4836032512 | bytes 1581056 | tf_op jit(solution)/shard_map/while/body/eval_jaxpr/dot_general | solution.py:68
  108.9 1.5 dynamic_update_slice.7
  110.4 0.9 constant_dynamic-slice_fusion.7
  112.2 10.0 %fusion.41 = f32[2048,96]{0,1:T(8,128)S(1)} fusion(f32[2048,96]{1,0:T(8,128)} %get-tuple-element.258, s32[2048]{0:T(1024)S(1)} %bitcast.95), kind=kOutput, calls=%fused_computation.3.clone.1 | convolution fusion | flops 4836032512 | bytes 1581056 | tf_op jit(solution)/shard_map/while/body/eval_jaxpr/dot_general | solution.py:68
  122.4 1.5 dynamic_update_slice.7
  123.9 0.9 constant_dynamic-slice_fusion.7
  125.8 10.0 %fusion.41 = f32[2048,96]{0,1:T(8,128)S(1)} fusion(f32[2048,96]{1,0:T(8,128)} %get-tuple-element.258, s32[2048]{0:T(1024)S(1)} %bitcast.95), kind=kOutput, calls=%fused_computation.3.clone.1 | convolution fusion | flops 4836032512 | bytes 1581056 | tf_op jit(solution)/shard_map/while/body/eval_jaxpr/dot_general | solution.py:68
  136.0 1.5 dynamic_update_slice.7
  137.5 0.9 constant_dynamic-slice_fusion.7
  138.4 0.9 constant_dynamic-slice_fusion.8
  139.3 10.0 %fusion.41 = f32[2048,96]{0,1:T(8,128)S(1)} fusion(f32[2048,96]{1,0:T(8,128)} %get-tuple-element.258, s32[2048]{0:T(1024)S(1)} %bitcast.95), kind=kOutput, calls=%fused_computation.3.clone.1 | convolution fusion | flops 4836032512 | bytes 1581056 | tf_op jit(solution)/shard_map/while/body/eval_jaxpr/dot_general | solution.py:68
  149.5 1.5 dynamic_update_slice.7
  151.1 0.9 constant_dynamic-slice_fusion.7
  152.0 0.9 constant_dynamic-slice_fusion.8
  152.9 10.0 %fusion.41 = f32[2048,96]{0,1:T(8,128)S(1)} fusion(f32[2048,96]{1,0:T(8,128)} %get-tuple-element.258, s32[2048]{0:T(1024)S(1)} %bitcast.95), kind=kOutput, calls=%fused_computation.3.clone.1 | convolution fusion | flops 4836032512 | bytes 1581056 | tf_op jit(solution)/shard_map/while/body/eval_jaxpr/dot_general | solution.py:68
  163.1 1.5 dynamic_update_slice.7
  164.6 0.9 constant_dynamic-slice_fusion.7
  166.4 10.0 %fusion.41 = f32[2048,96]{0,1:T(8,128)S(1)} fusion(f32[2048,96]{1,0:T(8,128)} %get-tuple-element.258, s32[2048]{0:T(1024)S(1)} %bitcast.95), kind=kOutput, calls=%fused_computation.3.clone.1 | convolution fusion | flops 4836032512 | bytes 1581056 | tf_op jit(solution)/shard_map/while/body/eval_jaxpr/dot_general | solution.py:68
  176.7 1.5 dynamic_update_slice.7
  178.2 0.9 constant_dynamic-slice_fusion.7
  180.0 10.0 %fusion.41 = f32[2048,96]{0,1:T(8,128)S(1)} fusion(f32[2048,96]{1,0:T(8,128)} %get-tuple-element.258, s32[2048]{0:T(1024)S(1)} %bitcast.95), kind=kOutput, calls=%fused_computation.3.clone.1 | convolution fusion | flops 4836032512 | bytes 1581056 | tf_op jit(solution)/shard_map/while/body/eval_jaxpr/dot_general | solution.py:68
  190.2 1.5 dynamic_update_slice.7
  191.7 0.9 constant_dynamic-slice_fusion.7
  193.5 10.0 %fusion.41 = f32[2048,96]{0,1:T(8,128)S(1)} fusion(f32[2048,96]{1,0:T(8,128)} %get-tuple-element.258, s32[2048]{0:T(1024)S(1)} %bitcast.95), kind=kOutput, calls=%fused_computation.3.clone.1 | convolution fusion | flops 4836032512 | bytes 1581056 | tf_op jit(solution)/shard_map/while/body/eval_jaxpr/dot_general | solution.py:68
  203.8 1.5 dynamic_update_slice.7
  205.3 1.6 reshape.148
  206.9 5.6 %all-to-all-start.4 = ((f32[32,1,512]{2,1,0:T(1,128)}), f32[32,1,512]{2,1,0:T(1,128)S(1)}, u32[]{:S(2)}, u32[]{:S(2)}) async-start(f32[32,1,512]{2,1,0:T(1,128)} %reshape.148), calls=%async_computation.4 | async-start | bytes 131072 | tf_op jit(solution)/shard_map/all_to_all | solution.py:121
  212.5 1.0 copy.191
  213.5 1.0 copy.192
  214.5 1.0 copy.193
  215.5 4.2 %all-to-all-done.4 = f32[32,1,512]{2,1,0:T(1,128)S(1)} async-done(((f32[32,1,512]{2,1,0:T(1,128)}), f32[32,1,512]{2,1,0:T(1,128)S(1)}, u32[]{:S(2)}, u32[]{:S(2)}) %all-to-all-start.4) | async-done | bytes 65568 | tf_op jit(solution)/shard_map/all_to_all | solution.py:121
  (120 shorter events, 17.4 us)
Async XLA Ops:
  4.7 23.8 %copy-start = (f32[3,32,16,128]{1,3,2,0:T(8,128)}, f32[3,32,16,128]{1,3,2,0:T(8,128)S(1)}, u32[]{:S(2)}) copy-start(f32[3,32,16,128]{1,3,2,0:T(8,128)S(1)} %copy.165) | copy-start | bytes 2359300
  4.7 14.0 %copy-start.7 = (s32[1,32,512]{2,1,0:T(8,128)S(1)}, s32[1,32,512]{2,1,0:T(8,128)}, u32[]{:S(2)}) copy-start(s32[1,32,512]{2,1,0:T(8,128)} %param.18) | copy-start | bytes 196612
  4.7 7.7 %collective-permute-start = (f32[3,32,1,128]{1,3,2,0:T(8,128)S(1)}, f32[3,32,1,128]{1,3,2,0:T(8,128)S(1)}, u32[]{:S(2)}, u32[]{:S(2)}) collective-permute-start(f32[3,32,1,128]{1,3,2,0:T(8,128)S(1)} %get-tuple-element.189), channel_id=1, source_target_pairs={{8,0},{16,8},{24,16},{0,24},{9,1},{17,9},{25,17},{1,25},{10,2},{18... | collective-permute-start | bytes 147464 | tf_op jit(solution)/shard_map/ppermute | solution.py:18
  7.1 6.3 %collective-permute-start.1 = (f32[3,32,1,128]{1,3,2,0:T(8,128)S(1)}, f32[3,32,1,128]{1,3,2,0:T(8,128)S(1)}, u32[]{:S(2)}, u32[]{:S(2)}) collective-permute-start(f32[3,32,1,128]{1,3,2,0:T(8,128)S(1)} %get-tuple-element.188), channel_id=1, source_target_pairs={{0,8},{8,16},{16,24},{24,0},{1,9},{9,17},{17,25},{25,1},{2,10},{10... | collective-permute-start | bytes 147464 | tf_op jit(solution)/shard_map/ppermute | solution.py:16
  14.1 11.4 %collective-permute-start.2 = (f32[3,32,18,1]{1,3,2,0:T(1,128)}, f32[3,32,18,1]{1,3,2,0:T(1,128)}, u32[]{:S(2)}, u32[]{:S(2)}) collective-permute-start(f32[3,32,18,1]{1,3,2,0:T(1,128)} %get-tuple-element.187), channel_id=1, source_target_pairs={{1,0},{2,1},{3,2},{4,3},{5,4},{6,5},{7,6},{0,7},{9,8},{10,9},{11,1... | collective-permute-start | bytes 20744 | tf_op jit(solution)/shard_map/ppermute | solution.py:18
  18.7 6.9 %collective-permute-start.3 = (f32[3,32,18,1]{1,3,2,0:T(1,128)}, f32[3,32,18,1]{1,3,2,0:T(1,128)}, u32[]{:S(2)}, u32[]{:S(2)}) collective-permute-start(f32[3,32,18,1]{1,3,2,0:T(1,128)} %get-tuple-element.186), channel_id=1, source_target_pairs={{0,1},{1,2},{2,3},{3,4},{4,5},{5,6},{6,7},{7,0},{8,9},{9,10},{10,1... | collective-permute-start | bytes 20744 | tf_op jit(solution)/shard_map/ppermute | solution.py:16
  19.4 19.9 %all-to-all-start = ((s32[1,32,512]{2,0,1:T(1,128)}), s32[1,32,512]{2,0,1:T(1,128)}, u32[]{:S(2)}, u32[]{:S(2)}) async-start(s32[1,32,512]{2,0,1:T(1,128)} %copy.182), calls=%async_computation | async-start | bytes 131072 | tf_op jit(solution)/shard_map/all_to_all | solution.py:115
  28.5 7.8 %copy-start.1 = (f32[1,32,16,128]{1,3,2,0:T(8,128)}, f32[1,32,16,128]{1,3,2,0:T(8,128)S(1)}, u32[]{:S(2)}) copy-start(f32[1,32,16,128]{1,3,2,0:T(8,128)S(1)} %fusion.32) | copy-start | bytes 786436
  36.3 2.3 %copy-start.8 = (s32[1,32,512]{2,1,0:T(8,128)S(1)}, s32[1,32,512]{2,1,0:T(8,128)}, u32[]{:S(2)}) copy-start(s32[1,32,512]{2,1,0:T(8,128)} %param.19) | copy-start | bytes 196612
  36.3 8.8 %copy-start.9 = (f32[1,32,512]{2,1,0:T(8,128)S(1)}, f32[1,32,512]{2,1,0:T(8,128)}, u32[]{:S(2)}) copy-start(f32[1,32,512]{2,1,0:T(8,128)} %param.21) | copy-start | bytes 196612
  37.2 21.9 %copy-start.13 = (f32[32]{0:T(128)S(1)}, f32[32]{0:T(128)}, u32[]{:S(2)}) copy-start(f32[32]{0:T(128)} %param.17) | copy-start | bytes 388
  37.2 8.7 %collective-permute-start.4 = (f32[4,32,1,128]{1,3,2,0:T(8,128)}, f32[4,32,1,128]{1,3,2,0:T(8,128)S(1)}, u32[]{:S(2)}, u32[]{:S(2)}) collective-permute-start(f32[4,32,1,128]{1,3,2,0:T(8,128)} %get-tuple-element.180), channel_id=1, source_target_pairs={{8,0},{16,8},{24,16},{0,24},{9,1},{17,9},{25,17},{1,25},{10,2},{18... | collective-permute-start | bytes 196616 | tf_op jit(solution)/shard_map/ppermute | solution.py:18
  38.6 7.8 %collective-permute-start.5 = (f32[4,32,1,128]{1,3,2,0:T(8,128)}, f32[4,32,1,128]{1,3,2,0:T(8,128)}, u32[]{:S(2)}, u32[]{:S(2)}) collective-permute-start(f32[4,32,1,128]{1,3,2,0:T(8,128)} %get-tuple-element.179), channel_id=1, source_target_pairs={{0,8},{8,16},{16,24},{24,0},{1,9},{9,17},{17,25},{25,1},{2,10},{10... | collective-permute-start | bytes 196616 | tf_op jit(solution)/shard_map/ppermute | solution.py:16
  39.3 13.8 %all-to-all-start.1 = ((s32[1,32,512]{2,0,1:T(1,128)}), s32[1,32,512]{2,0,1:T(1,128)S(1)}, u32[]{:S(2)}, u32[]{:S(2)}) async-start(s32[1,32,512]{2,0,1:T(1,128)} %copy.184), calls=%async_computation.1 | async-start | bytes 131072 | tf_op jit(solution)/shard_map/all_to_all | solution.py:116
  48.0 32.0 %collective-permute-start.6 = (f32[4,32,18,1]{1,0,3,2:T(4,128)}, f32[4,32,18,1]{1,0,3,2:T(4,128)}, u32[]{:S(2)}, u32[]{:S(2)}) collective-permute-start(f32[4,32,18,1]{1,0,3,2:T(4,128)} %copy.170), channel_id=1, source_target_pairs={{1,0},{2,1},{3,2},{4,3},{5,4},{6,5},{7,6},{0,7},{9,8},{10,9},{11,1... | collective-permute-start | bytes 27656 | tf_op jit(solution)/shard_map/ppermute | solution.py:18
  53.1 27.8 %collective-permute-start.7 = (f32[4,32,18,1]{1,0,3,2:T(4,128)}, f32[4,32,18,1]{1,0,3,2:T(4,128)}, u32[]{:S(2)}, u32[]{:S(2)}) collective-permute-start(f32[4,32,18,1]{1,0,3,2:T(4,128)} %copy.172), channel_id=1, source_target_pairs={{0,1},{1,2},{2,3},{3,4},{4,5},{5,6},{6,7},{7,0},{8,9},{9,10},{10,1... | collective-permute-start | bytes 27656 | tf_op jit(solution)/shard_map/ppermute | solution.py:16
  53.1 20.0 %all-to-all-start.2 = ((f32[1,32,512]{2,0,1:T(1,128)}), f32[1,32,512]{2,0,1:T(1,128)S(1)}, u32[]{:S(2)}, u32[]{:S(2)}) async-start(f32[1,32,512]{2,0,1:T(1,128)} %copy.185), calls=%async_computation.2 | async-start | bytes 131072 | tf_op jit(solution)/shard_map/all_to_all | solution.py:118
  73.1 22.6 %all-to-all-start.3 = ((f32[1,32,3,512]{3,2,0,1:T(4,128)}), f32[1,32,3,512]{3,2,0,1:T(4,128)}, u32[]{:S(2)}, u32[]{:S(2)}) async-start(f32[1,32,3,512]{3,2,0,1:T(4,128)} %copy.186), calls=%async_computation.3 | async-start | bytes 524288 | tf_op jit(solution)/shard_map/all_to_all | solution.py:117
  81.7 4.5 %copy-start.2 = (f32[1,32,16,128]{1,3,2,0:T(8,128)S(1)}, f32[1,32,16,128]{1,3,2,0:T(8,128)}, u32[]{:S(2)}) copy-start(f32[1,32,16,128]{1,3,2,0:T(8,128)} %copy-done.1) | copy-start | bytes 786436
  87.2 3.3 %copy-start.3 = (f32[32,18,130]{0,2,1:T(8,128)S(1)}, f32[32,18,130]{0,2,1:T(8,128)}, u32[]{:S(2)}) copy-start(f32[32,18,130]{0,2,1:T(8,128)} %get-tuple-element.182) | copy-start | bytes 898564
  87.2 3.3 %copy-start.4 = (f32[32,16,128]{0,2,1:T(8,128)S(1)}, f32[32,16,128]{0,2,1:T(8,128)}, u32[]{:S(2)}) copy-start(f32[32,16,128]{0,2,1:T(8,128)} %copy.174) | copy-start | bytes 786436
  87.2 3.3 %copy-start.5 = (f32[32,16,128]{0,2,1:T(8,128)S(1)}, f32[32,16,128]{0,2,1:T(8,128)}, u32[]{:S(2)}) copy-start(f32[32,16,128]{0,2,1:T(8,128)} %copy.175) | copy-start | bytes 786436
  87.2 3.3 %copy-start.6 = (f32[32,16,128]{0,2,1:T(8,128)S(1)}, f32[32,16,128]{0,2,1:T(8,128)}, u32[]{:S(2)}) copy-start(f32[32,16,128]{0,2,1:T(8,128)} %copy.176) | copy-start | bytes 786436
  87.2 3.3 %copy-start.12 = (f32[32]{0:T(128)S(1)}, f32[32]{0:T(128)}, u32[]{:S(2)}) copy-start(f32[32]{0:T(128)} %param.16) | copy-start | bytes 388
  205.3 14.5 %copy-start.10 = (f32[1,32,512]{2,1,0:T(8,128)S(1)}, f32[1,32,512]{2,1,0:T(8,128)}, u32[]{:S(2)}) copy-start(f32[1,32,512]{2,1,0:T(8,128)} %param.22) | copy-start | bytes 196612
  205.3 14.5 %copy-start.11 = (s32[1,32,512]{2,1,0:T(8,128)S(1)}, s32[1,32,512]{2,1,0:T(8,128)}, u32[]{:S(2)}) copy-start(s32[1,32,512]{2,1,0:T(8,128)} %param.23) | copy-start | bytes 196612
  206.9 12.9 %all-to-all-start.4 = ((f32[32,1,512]{2,1,0:T(1,128)}), f32[32,1,512]{2,1,0:T(1,128)S(1)}, u32[]{:S(2)}, u32[]{:S(2)}) async-start(f32[32,1,512]{2,1,0:T(1,128)} %reshape.148), calls=%async_computation.4 | async-start | bytes 131072 | tf_op jit(solution)/shard_map/all_to_all | solution.py:121
where the time goes:
time: 223 us; the launch traced here: 221 us
  matrix products  80.3 us (36%)
  local copies, waits for them, and re-layouts  56 us (25%)
  starting transfers between devices  42.5 us (19%)
  other arithmetic  29.2 us (13%)
  waiting for transfers between devices  11.2 us (5%)
    dot_general x8, matrix products, one_block(): jnp.dot(onehot, table, preferred_element_type=jnp.float32, precision=lax....  80.3 us
    unnamed x40, local copies, waits for them, and re-layouts  16.9 us
    dynamic_slice x24, local copies, waits for them, and re-layouts, interpolate(): model = lax.map(one_block, (flat_cells, flat_levels, flat_vfrac, flat_bary))  14.1 us
    ppermute x4, starting transfers between devices, padded(): lax.ppermute(head, axis, [((i + 1) % count, i) for i in range(count)])  12.9 us
    dynamic_update_slice x8, local copies, waits for them, and re-layouts, interpolate(): model = lax.map(one_block, (flat_cells, flat_levels, flat_vfrac, flat_bary))  12 us
    concatenate x5, other arithmetic, padded(): jnp.concatenate([lax.ppermute(tail, axis, [(i, (i + 1) % count) for i in...  10.1 us
    sub x2, other arithmetic, laplace(): return total - 6.0 * inner_view(field, 0, 0)  8.35 us
    all_to_all x1, starting transfers between devices, on_device(): lax.all_to_all(obs_bary, ('px', 'py'), split_axis=1, concat_axis=0, tiled...  6.14 us
  transfers between devices with their start and end apart: 13, of which 4 were waited for; matrix products, arithmetic and copies ran while one was open for 22% of the time, Pallas kernels for 0%

commit v1 on v0

v1 whole, which is shorter than its diff:
```python
import functools

import jax
import jax.numpy as jnp
from jax import lax
from jax.experimental import pallas as pl
from jax.experimental.pallas import tpu as pltpu
from jax.sharding import PartitionSpec as P

MESH = pl.DeviceIdType.MESH
FIELDS = 5
CORNERS = ((-1, -1), (-1, 1), (1, -1), (1, 1))


def laplace(x):
    rows, cols = x.shape
    below = pltpu.roll(x, rows - 1, 0)
    above = pltpu.roll(x, 1, 0)
    return (
        below
        + above
        + pltpu.roll(x + above, cols - 1, 1)
        + pltpu.roll(x + below, 1, 1)
        - 6.0 * x
    )


def diff_x(x):
    return (pltpu.roll(x, x.shape[0] - 1, 0) - pltpu.roll(x, 1, 0)) * 0.5


def diff_y(x):
    return (pltpu.roll(x, x.shape[1] - 1, 1) - pltpu.roll(x, 1, 1)) * 0.5


def kernel(
    sizes,
    hyper,
    damp,
    u_ref,
    v_ref,
    t_ref,
    cells_ref,
    levels_ref,
    bary_ref,
    vfrac_ref,
    values_ref,
    mask_ref,
    u_out,
    v_out,
    t_out,
    dep_out,
    out_buf,
    in_buf,
    model_buf,
    model_in,
    row_buf,
    row_in,
    col_buf,
    col_in,
    corner_in,
    table,
    obs_send,
    obs_recv,
    model_send,
    model_recv,
    halo_send,
    halo_recv,
):
    n_px, n_py, tiles = sizes
    count = n_px * n_py
    levs, rows, cols = t_ref.shape
    px = lax.axis_index("px")
    py = lax.axis_index("py")
    me = px * n_py + py
    fields = (u_ref, v_ref, t_ref)

    def place(dev):
        return (dev // n_py, dev % n_py)

    barrier = pltpu.get_barrier_semaphore()

    def greet(k, _):
        pl.semaphore_signal(
            barrier, inc=1, device_id=place(lax.rem(me + k, count)), device_id_type=MESH
        )
        return 0

    lax.fori_loop(1, count, greet, 0)

    row8 = lax.broadcasted_iota(jnp.int32, (8, cols), 0)
    lane16 = lax.broadcasted_iota(jnp.int32, (rows, cols), 1)
    lane24 = lax.broadcasted_iota(jnp.int32, (rows + 8, cols), 1)

    def pack_edges(g, _):
        edge = jnp.zeros((rows, cols), jnp.float32)
        for f, ref in enumerate(fields):
            for half in range(2):
                top = jnp.zeros((8, cols), jnp.float32)
                bottom = top
                for i in range(4):
                    at = half * 4 + i
                    x = ref[g * 8 + at]
                    base = 16 * at + 4 * f
                    edge = jnp.where(
                        lane16 // 4 == base // 4, pltpu.roll(x, (base + 2) % cols, 1), edge
                    )
                    here = row8 // 2 == i
                    head = x[:8]
                    tail = x[rows - 8 :]
                    if i:
                        head = pltpu.roll(head, 2 * i, 0)
                    if (2 * i + 2) % 8:
                        tail = pltpu.roll(tail, 2 * i + 2, 0)
                    top = jnp.where(here, head, top)
                    bottom = jnp.where(here, tail, bottom)
                row_buf[0, f, g * 2 + half] = top
                row_buf[1, f, g * 2 + half] = bottom
        col_buf[g] = edge
        return 0

    lax.fori_loop(0, levs // 8, pack_edges, 0)

    def pack_obs(g, _):
        lines = pl.ds(pl.multiple_of(g * 8, 8), 8)
        for t in range(tiles):
            part = pl.ds(t * 128, 128)
            whole = (
                cells_ref[0, lines, part].astype(jnp.float32),
                levels_ref[0, lines, part].astype(jnp.float32),
                vfrac_ref[0, lines, part],
            )
            for i in range(8):
                for f, x in enumerate(whole):
                    out_buf[g * 8 + i, f, pl.ds(t, 1)] = x[i : i + 1]
                for j in range(2):
                    out_buf[g * 8 + i, 3 + j, pl.ds(t, 1)] = bary_ref[0, g * 8 + i, pl.ds(j, 1), part]
        return 0

    lax.fori_loop(0, count // 8, pack_obs, 0)
    in_buf[me] = out_buf[me]

    pl.semaphore_wait(barrier, count - 1)

    def remote(src, dst, send, recv, dev):
        return pltpu.make_async_remote_copy(
            src_ref=src,
            dst_ref=dst,
            send_sem=send,
            recv_sem=recv,
            device_id=dev,
            device_id_type=MESH,
        )

    up = lax.rem(px + n_px - 1, n_px)
    down = lax.rem(px + 1, n_px)
    left = lax.rem(py + n_py - 1, n_py)
    right = lax.rem(py + 1, n_py)
    halo = []

    def edge_copy(src, dst, dev):
        k = len(halo)
        halo.append(remote(src, dst, halo_send.at[k], halo_recv.at[k], dev))

    edge_copy(row_buf.at[0], row_in.at[0], (up, py))
    edge_copy(row_buf.at[1], row_in.at[1], (down, py))
    edge_copy(col_buf, col_in.at[0], (px, left))
    edge_copy(col_buf, col_in.at[1], (px, right))
    for k, (step_x, step_y) in enumerate(CORNERS):
        part = pl.ds(0, 8) if step_x < 0 else pl.ds(rows - 8, 8)
        edge_copy(
            col_buf.at[:, part],
            corner_in.at[k],
            (up if step_x < 0 else down, left if step_y < 0 else right),
        )
    for copy in halo:
        copy.start()

    def obs_copy(k):
        dev = lax.rem(me + k, count)
        return remote(
            out_buf.at[dev], in_buf.at[me], obs_send.at[dev], obs_recv.at[me], place(dev)
        )

    def send_obs(k, _):
        obs_copy(k).start()
        return 0

    lax.fori_loop(1, count, send_obs, 0)
    for copy in halo:
        copy.wait()

    def advance(g, _):
        low = row8 < 4
        from_left = jnp.concatenate(
            [col_in[1, g // 2], jnp.where(low, corner_in[1, g // 2], corner_in[3, g // 2])], axis=0
        )
        from_right = jnp.concatenate(
            [col_in[0, g // 2], jnp.where(low, corner_in[0, g // 2], corner_in[2, g // 2])], axis=0
        )
        sides = jnp.where(lane24 % 4 < 2, from_left, from_right)
        sides = pltpu.roll(sides, 64 * (g % 2), 1)
        for i in range(4):
            lev = g * 4 + i
            whole = []
            for f, ref in enumerate(fields):
                below = row_in[0, f, g]
                above = row_in[1, f, g]
                if i:
                    below = pltpu.roll(below, 8 - 2 * i, 0)
                if (6 - 2 * i) % 8:
                    above = pltpu.roll(above, 6 - 2 * i, 0)
                middle = jnp.concatenate([ref[lev], jnp.where(low, below, above)], axis=0)
                base = 16 * i + 4 * f
                edge = pltpu.roll(sides, (2 * cols - base - 2) % cols, 1)
                whole.append(jnp.concatenate([middle, edge], axis=1))
            u, v, t = whole
            coef = hyper[lev]
            rate = damp[lev]
            div = diff_x(u) + diff_y(v)
            u_in = u[:rows, :cols]
            v_in = v[:rows, :cols]
            t_in = t[:rows, :cols]
            u_out[lev] = (
                u_in
                - coef * laplace(laplace(u))[:rows, :cols]
                + rate * diff_x(div)[:rows, :cols]
            )
            v_out[lev] = (
                v_in
                - coef * laplace(laplace(v))[:rows, :cols]
                + rate * diff_y(div)[:rows, :cols]
            )
            drift = u_in * diff_x(t)[:rows, :cols] + v_in * diff_y(t)[:rows, :cols]
            t_out[lev] = t_in - coef * laplace(laplace(t))[:rows, :cols] - 0.5 * drift
        return 0

    lax.fori_loop(0, levs // 4, advance, 0)

    for r in range(rows):
        line = t_out[:, r, :]
        for step in range(2):
            if step:
                line = pltpu.roll(line, cols - 1, 1)
            high = line.astype(jnp.bfloat16)
            low = (line - high.astype(jnp.float32)).astype(jnp.bfloat16)
            at = (r * 2 + step) * levs
            table[pl.ds(at, levs), pl.ds(0, cols)] = high
            table[pl.ds(at, levs), pl.ds(cols, cols)] = low

    group = 2 if tiles % 2 == 0 else 1
    width = group * 128
    col_iota = lax.broadcasted_iota(jnp.int32, (cols, width), 0)
    lev_iota = lax.broadcasted_iota(jnp.int32, (levs, width), 0)

    def interpolate(k, _):
        src = lax.rem(me + count - k, count)

        @pl.when(k > 0)
        def _():
            remote(
                out_buf.at[src], in_buf.at[src], obs_send.at[src], obs_recv.at[src], place(src)
            ).wait_recv()

        for part in range(tiles // group):

            def piece(f):
                return jnp.concatenate(
                    [in_buf[src, f, pl.ds(part * group + t, 1)] for t in range(group)], axis=1
                )

            cell = piece(0).astype(jnp.int32)
            level = piece(1).astype(jnp.int32)
            frac = piece(2)
            w0 = piece(3)
            w1 = piece(4)
            w2 = 1.0 - w0 - w1
            col = cell & (cols - 1)
            row = cell // cols
            hot = jnp.where(col_iota == col, 1.0, 0.0).astype(jnp.bfloat16)
            hot = jnp.concatenate([hot, hot], axis=0)
            found = jnp.dot(table[...], hot, preferred_element_type=jnp.float32)
            zero = jnp.zeros((levs, width), jnp.float32)
            base, nxt, side = zero, zero, zero
            before = None
            for r in range(rows):
                at = r * 2 * levs
                line = found[at : at + levs]
                if before is not None:
                    nxt = jnp.where(before, line, nxt)
                if r < rows - 1:
                    here = jnp.broadcast_to(row == r, (levs, width))
                    base = jnp.where(here, line, base)
                    side = jnp.where(here, found[at + levs : at + 2 * levs], side)
                    before = here
            column = w0 * base + w1 * nxt + w2 * side
            share = jnp.where(lev_iota == level, 1.0 - frac, 0.0)
            share = jnp.where(lev_iota == level + 1, frac, share)
            model = jnp.sum(column * share, axis=0, keepdims=True)
            for t in range(group):
                model_buf[src, pl.ds(part * group + t, 1)] = model[:, t * 128 : (t + 1) * 128]

        @pl.when(k > 0)
        def _():
            remote(
                model_buf.at[src],
                model_in.at[me],
                model_send.at[src],
                model_recv.at[me],
                place(src),
            ).start()

        return 0

    lax.fori_loop(0, count, interpolate, 0)
    model_in[me] = model_buf[me]

    def finish(k, _):
        dev = lax.rem(me + count - k, count)

        obs_copy(k).wait_send()
        remote(
            model_buf.at[dev],
            model_in.at[dev],
            model_send.at[dev],
            model_recv.at[dev],
            place(dev),
        ).wait()
        return 0

    lax.fori_loop(1, count, finish, 0)

    def depart(g, _):
        lines = pl.ds(pl.multiple_of(g * 8, 8), 8)
        for t in range(tiles):
            part = pl.ds(t * 128, 128)
            model = jnp.concatenate(
                [model_in[g * 8 + i, pl.ds(t, 1)] for i in range(8)], axis=0
            )
            dep_out[0, lines, part] = mask_ref[0, lines, part].astype(jnp.float32) * (
                values_ref[0, lines, part] - model
            )
        return 0

    lax.fori_loop(0, count // 8, depart, 0)


def solution(mesh):
    n_px = mesh.shape["px"]
    n_py = mesh.shape["py"]
    count = n_px * n_py

    def on_device(
        theta_field,
        wind_u,
        wind_v,
        hyper_coef,
        damp_coef,
        obs_cells,
        obs_levels,
        obs_bary,
        obs_vfrac,
        obs_values,
        obs_mask,
    ):
        levs, rows, cols = theta_field.shape
        tiles = obs_values.shape[2] // 128
        vmem = pl.BlockSpec(memory_space=pltpu.VMEM)
        smem = pl.BlockSpec(memory_space=pltpu.SMEM)
        f32 = jnp.float32
        field = jax.ShapeDtypeStruct(theta_field.shape, f32)
        u_next, v_next, t_next, dep = pl.pallas_call(
            functools.partial(kernel, (n_px, n_py, tiles)),
            out_shape=(field, field, field, jax.ShapeDtypeStruct(obs_values.shape, f32)),
            in_specs=[smem] * 2 + [vmem] * 9,
            out_specs=[vmem] * 4,
            scratch_shapes=[
                pltpu.VMEM((count, FIELDS, tiles, 128), f32),
                pltpu.VMEM((count, FIELDS, tiles, 128), f32),
                pltpu.VMEM((count, tiles, 128), f32),
                pltpu.VMEM((count, tiles, 128), f32),
                pltpu.VMEM((2, 3, levs // 4, 8, cols), f32),
                pltpu.VMEM((2, 3, levs // 4, 8, cols), f32),
                pltpu.VMEM((levs // 8, rows, cols), f32),
                pltpu.VMEM((2, levs // 8, rows, cols), f32),
                pltpu.VMEM((4, levs // 8, 8, cols), f32),
                pltpu.VMEM((rows * 2 * levs, 2 * cols), jnp.bfloat16),
                pltpu.SemaphoreType.DMA((count,)),
                pltpu.SemaphoreType.DMA((count,)),
                pltpu.SemaphoreType.DMA((count,)),
                pltpu.SemaphoreType.DMA((count,)),
                pltpu.SemaphoreType.DMA((8,)),
                pltpu.SemaphoreType.DMA((8,)),
            ],
            compiler_params=pltpu.CompilerParams(
                collective_id=0, has_side_effects=True, vmem_limit_bytes=40 * 1024 * 1024
            ),
        )(
            hyper_coef,
            damp_coef,
            wind_u,
            wind_v,
            theta_field,
            obs_cells,
            obs_levels,
            obs_bary,
            obs_vfrac,
            obs_values,
            obs_mask,
        )
        return (t_next, u_next, v_next, dep)

    cells = P(None, "px", "py")
    obs = P(("px", "py"), None, None)
    return jax.shard_map(
        on_device,
        mesh=mesh,
        in_specs=(cells, cells, cells, P(), P(), obs, obs, P(("px", "py"), None, None, None), obs, obs, obs),
        out_specs=(cells, cells, cells, obs),
        check_vma=False,
    )
```

time: 223 us -> 51.2 us (0.23)
  matrix products: 80.3 us -> 0 us
  local copies, waits for them, and re-layouts: 56 us -> 8.76 us
  starting transfers between devices: 42.5 us -> 0 us
  Pallas kernels: 0 us -> 41.4 us
  other arithmetic: 29.2 us -> 0 us
  waiting for transfers between devices: 11.2 us -> 0 us
    dot_general x8 -> x0, matrix products: 80.3 us -> none  [one_block(): jnp.dot(onehot, table, preferred_element_type=jnp.float32, precision=lax....]
    pallas_call x0 -> x1, Pallas kernels: none -> 41.4 us  [on_device(): pl.pallas_call(functools.partial(kernel, (n_px, n_py, tiles)), out_shape=...]
    all_to_all x5 -> x0, starting transfers between devices: 29.6 us -> none  [the longest x1 6.14 us: on_device(): lax.all_to_all(obs_bary, ('px', 'py'), split_axis=1, concat_axis=0, tiled...]
    dynamic_slice x24 -> x0, local copies, waits for them, and re-layouts: 14.1 us -> none  [interpolate(): model = lax.map(one_block, (flat_cells, flat_levels, flat_vfrac, flat_bary))]
    ppermute x8 -> x0, starting transfers between devices: 12.9 us -> none  [the longest x4 12.9 us: padded(): lax.ppermute(head, axis, [((i + 1) % count, i) for i in range(count)])]
    dynamic_update_slice x8 -> x0, local copies, waits for them, and re-layouts: 12 us -> none  [interpolate(): model = lax.map(one_block, (flat_cells, flat_levels, flat_vfrac, flat_bary))]
    concatenate x7 -> x0, other arithmetic: 11.9 us -> none  [the longest x5 10.1 us: padded(): jnp.concatenate([lax.ppermute(tail, axis, [(i, (i + 1) % count) for i in...]
    sub x10 -> x0, other arithmetic: 8.4 us -> none  [the longest x2 8.35 us: laplace(): return total - 6.0 * inner_view(field, 0, 0)]
  transfers between devices with their start and end apart: 13 -> 0, of which waited for: 4 -> 0; matrix products, arithmetic and copies ran while one was open for 22% -> 0% of each run, Pallas kernels for 0% -> 0%
where the time goes in v1:
time: 51.2 us; the launch traced here: 50.9 us
  Pallas kernels  41.4 us (81%)
  local copies, waits for them, and re-layouts  8.76 us (17%)
  between operations  0.72 us (1%)
    pallas_call x1, Pallas kernels, on_device(): pl.pallas_call(functools.partial(kernel, (n_px, n_py, tiles)), out_shape=...  41.4 us
    unnamed x25, local copies, waits for them, and re-layouts  8.76 us

profile of v1, /device:TPU:0, one launch (start us, length us, event | category | flops | bytes accessed | tf_op | source)
XLA Modules:
  0.0 50.9 jit_solution(9344318104331077984)
XLA Ops:
  0.6 0.0 copy-start.5
  0.6 0.0 copy-start.4
  0.7 0.0 copy-start.3
  0.7 0.0 copy-start
  0.7 1.1 %copy.15.bary_ref = f32[1,32,3,512]{3,2,1,0:T(4,128)S(1)} copy(f32[1,32,3,512]{3,1,2,0:T(8,128)} %param.18) | data formatting | bytes 393216 | tf_op args[7]
  1.8 0.0 copy-done.5
  1.8 0.0 copy-done.4
  1.8 0.0 copy-done.3
  1.8 0.0 copy-done
  1.8 0.0 copy-start.1
  1.8 0.9 %copy-done.1 = f32[32,16,128]{2,1,0:T(8,128)S(1)} copy-done((f32[32,16,128]{2,1,0:T(8,128)S(1)}, f32[32,16,128]{2,1,0:T(8,128)}, u32[]{:S(2)}) %copy-start.1) | copy-done | bytes 262168
  2.8 0.0 copy-start.2
  2.8 0.9 %copy-done.2 = f32[32,16,128]{2,1,0:T(8,128)S(1)} copy-done((f32[32,16,128]{2,1,0:T(8,128)S(1)}, f32[32,16,128]{2,1,0:T(8,128)}, u32[]{:S(2)}) %copy-start.2) | copy-done | bytes 262168
  3.7 0.0 copy-start.6
  3.7 0.8 %copy-done.6 = f32[1,32,512]{2,1,0:T(8,128)S(1)} copy-done((f32[1,32,512]{2,1,0:T(8,128)S(1)}, f32[1,32,512]{2,1,0:T(8,128)}, u32[]{:S(2)}) %copy-start.6) | copy-done | bytes 65560
  4.6 0.0 copy-start.7
  4.6 0.8 %copy-done.7 = s32[1,32,512]{2,1,0:T(8,128)S(1)} copy-done((s32[1,32,512]{2,1,0:T(8,128)S(1)}, s32[1,32,512]{2,1,0:T(8,128)}, u32[]{:S(2)}) %copy-start.7) | copy-done | bytes 65560
  5.4 0.0 copy-start.8
  5.4 0.7 %copy-done.8 = f32[32]{0:T(128)S(1)} copy-done((f32[32]{0:T(128)S(1)}, f32[32]{0:T(128)}, u32[]{:S(2)}) %copy-start.8) | copy-done | bytes 152
  6.1 0.0 copy-start.9
  6.1 0.7 %copy-done.9 = f32[32]{0:T(128)S(1)} copy-done((f32[32]{0:T(128)S(1)}, f32[32]{0:T(128)}, u32[]{:S(2)}) %copy-start.9) | copy-done | bytes 152
  6.7 41.4 %shard_map.138 = (f32[32,16,128]{2,1,0:T(8,128)S(1)}, f32[32,16,128]{2,1,0:T(8,128)S(1)}, f32[32,16,128]{2,1,0:T(8,128)S(1)}, f32[1,32,512]{2,1,0:T(8,128)S(1)}) custom-call(f32[32]{0:T(128)S(1)} %copy-done.8, f32[32]{0:T(128)S(1)} %copy-done.9, f32[32,16,128]{2,1,0:T(8,128)S(1)} %copy-done, f32[32,16,128]{2,1,0:T(8,128)S(1)} %copy-done.1, ...), custom_call_target="tpu_custom_call" | custom-call | tf_op jit(solution)/shard_map/pallas_call | solution.py:372
  48.2 0.7 %copy.20 = f32[32,16,128]{2,1,0:T(8,128)} copy(f32[32,16,128]{2,1,0:T(8,128)S(1)} %get-tuple-element.16) | data formatting | bytes 524288
  48.9 0.7 %copy.21 = f32[32,16,128]{2,1,0:T(8,128)} copy(f32[32,16,128]{2,1,0:T(8,128)S(1)} %get-tuple-element.17) | data formatting | bytes 524288
  49.6 0.7 %copy.22 = f32[32,16,128]{2,1,0:T(8,128)} copy(f32[32,16,128]{2,1,0:T(8,128)S(1)} %get-tuple-element.18) | data formatting | bytes 524288
  50.3 0.6 %copy.23 = f32[1,32,512]{2,1,0:T(8,128)} copy(f32[1,32,512]{2,1,0:T(8,128)S(1)} %get-tuple-element.19) | data formatting | bytes 131072
Async XLA Ops:
  0.6 1.2 %copy-start.5 = (f32[1,32,512]{2,1,0:T(8,128)S(1)}, f32[1,32,512]{2,1,0:T(8,128)}, u32[]{:S(2)}) copy-start(f32[1,32,512]{2,1,0:T(8,128)} %vfrac_ref.1) | copy-start | bytes 196612
  0.6 1.2 %copy-start.4 = (s32[1,32,512]{2,1,0:T(8,128)S(1)}, s32[1,32,512]{2,1,0:T(8,128)}, u32[]{:S(2)}) copy-start(s32[1,32,512]{2,1,0:T(8,128)} %levels_ref.1) | copy-start | bytes 196612
  0.7 1.2 %copy-start.3 = (s32[1,32,512]{2,1,0:T(8,128)S(1)}, s32[1,32,512]{2,1,0:T(8,128)}, u32[]{:S(2)}) copy-start(s32[1,32,512]{2,1,0:T(8,128)} %cells_ref.1) | copy-start | bytes 196612
  0.7 1.2 %copy-start = (f32[32,16,128]{2,1,0:T(8,128)S(1)}, f32[32,16,128]{2,1,0:T(8,128)}, u32[]{:S(2)}) copy-start(f32[32,16,128]{2,1,0:T(8,128)} %u_ref.1) | copy-start | bytes 786436
  1.8 1.0 %copy-start.1 = (f32[32,16,128]{2,1,0:T(8,128)S(1)}, f32[32,16,128]{2,1,0:T(8,128)}, u32[]{:S(2)}) copy-start(f32[32,16,128]{2,1,0:T(8,128)} %v_ref.1) | copy-start | bytes 786436
  2.8 0.9 %copy-start.2 = (f32[32,16,128]{2,1,0:T(8,128)S(1)}, f32[32,16,128]{2,1,0:T(8,128)}, u32[]{:S(2)}) copy-start(f32[32,16,128]{2,1,0:T(8,128)} %t_ref.1) | copy-start | bytes 786436
  3.7 0.8 %copy-start.6 = (f32[1,32,512]{2,1,0:T(8,128)S(1)}, f32[1,32,512]{2,1,0:T(8,128)}, u32[]{:S(2)}) copy-start(f32[1,32,512]{2,1,0:T(8,128)} %values_ref.1) | copy-start | bytes 196612
  4.6 0.8 %copy-start.7 = (s32[1,32,512]{2,1,0:T(8,128)S(1)}, s32[1,32,512]{2,1,0:T(8,128)}, u32[]{:S(2)}) copy-start(s32[1,32,512]{2,1,0:T(8,128)} %mask_ref.1) | copy-start | bytes 196612
  5.4 0.7 %copy-start.8 = (f32[32]{0:T(128)S(1)}, f32[32]{0:T(128)}, u32[]{:S(2)}) copy-start(f32[32]{0:T(128)} %hyper.1) | copy-start | bytes 388
  6.1 0.7 %copy-start.9 = (f32[32]{0:T(128)S(1)}, f32[32]{0:T(128)}, u32[]{:S(2)}) copy-start(f32[32]{0:T(128)} %damp.1) | copy-start | bytes 388

commit v2 on v1

--- a/solution.py
+++ b/solution.py
@@ -37,6 +37,19 @@
     sizes,
     hyper,
     damp,
+    u_hbm,
+    v_hbm,
+    t_hbm,
+    cells_hbm,
+    levels_hbm,
+    bary_hbm,
+    vfrac_hbm,
+    values_hbm,
+    mask_hbm,
+    u_res,
+    v_res,
+    t_res,
+    dep_res,
     u_ref,
     v_ref,
     t_ref,
@@ -66,6 +79,8 @@
     model_recv,
     halo_send,
     halo_recv,
+    load_sem,
+    store_sem,
 ):
     n_px, n_py, tiles = sizes
     count = n_px * n_py
@@ -78,6 +93,25 @@
     def place(dev):
         return (dev // n_py, dev % n_py)
 
+    loads = [
+        pltpu.make_async_copy(src, dst, load_sem.at[k])
+        for k, (src, dst) in enumerate(
+            (
+                (u_hbm, u_ref),
+                (v_hbm, v_ref),
+                (t_hbm, t_ref),
+                (cells_hbm, cells_ref),
+                (levels_hbm, levels_ref),
+                (vfrac_hbm, vfrac_ref),
+                (bary_hbm, bary_ref),
+                (values_hbm, values_ref),
+                (mask_hbm, mask_ref),
+            )
+        )
+    ]
+    for load in loads:
+        load.start()
+
     barrier = pltpu.get_barrier_semaphore()
 
     def greet(k, _):
@@ -91,6 +125,9 @@
     row8 = lax.broadcasted_iota(jnp.int32, (8, cols), 0)
     lane16 = lax.broadcasted_iota(jnp.int32, (rows, cols), 1)
     lane24 = lax.broadcasted_iota(jnp.int32, (rows + 8, cols), 1)
+
+    for load in loads[:3]:
+        load.wait()
 
     def pack_edges(g, _):
         edge = jnp.zeros((rows, cols), jnp.float32)
@@ -121,6 +158,9 @@
 
     lax.fori_loop(0, levs // 8, pack_edges, 0)
 
+    for load in loads[3:]:
+        load.wait()
+
     def pack_obs(g, _):
         lines = pl.ds(pl.multiple_of(g * 8, 8), 8)
         for t in range(tiles):
@@ -129,12 +169,12 @@
                 cells_ref[0, lines, part].astype(jnp.float32),
                 levels_ref[0, lines, part].astype(jnp.float32),
                 vfrac_ref[0, lines, part],
+                bary_ref[0, 0, lines, part],
+                bary_ref[0, 1, lines, part],
             )
             for i in range(8):
                 for f, x in enumerate(whole):
                     out_buf[g * 8 + i, f, pl.ds(t, 1)] = x[i : i + 1]
-                for j in range(2):
-                    out_buf[g * 8 + i, 3 + j, pl.ds(t, 1)] = bary_ref[0, g * 8 + i, pl.ds(j, 1), part]
         return 0
 
     lax.fori_loop(0, count // 8, pack_obs, 0)
@@ -236,6 +276,14 @@
         return 0
 
     lax.fori_loop(0, levs // 4, advance, 0)
+    stores = [
+        pltpu.make_async_copy(src, dst, store_sem.at[k])
+        for k, (src, dst) in enumerate(
+            ((u_out, u_res), (v_out, v_res), (t_out, t_res), (dep_out, dep_res))
+        )
+    ]
+    for store in stores[:3]:
+        store.start()
 
     for r in range(rows):
         line = t_out[:, r, :]
@@ -248,71 +296,92 @@
             table[pl.ds(at, levs), pl.ds(0, cols)] = high
             table[pl.ds(at, levs), pl.ds(cols, cols)] = low
 
-    group = 2 if tiles % 2 == 0 else 1
-    width = group * 128
+    chunks = max(1, tiles // 2)
+    width = 256
+    step_rows = 2 * levs
     col_iota = lax.broadcasted_iota(jnp.int32, (cols, width), 0)
     lev_iota = lax.broadcasted_iota(jnp.int32, (levs, width), 0)
 
-    def interpolate(k, _):
+    def piece(src, f, j):
+        return jnp.concatenate(
+            [in_buf[src, f, pl.ds(min(j * 2 + t, tiles - 1), 1)] for t in range(2)], axis=1
+        )
+
+    def stage(k):
         src = lax.rem(me + count - k, count)
-
-        @pl.when(k > 0)
-        def _():
+        for j in range(chunks):
+            col = piece(src, 0, j).astype(jnp.int32) & (cols - 1)
+            hot = jnp.where(col_iota == col, 1.0, 0.0).astype(jnp.bfloat16)
+            pltpu.matmul_push_rhs(jnp.concatenate([hot, hot], axis=0), 0, j)
+
+    def run(accs):
+        def feed(j, r):
+            pltpu.matmul_acc_lhs(
+                accs[j][r],
+                table[pl.ds(r * step_rows, step_rows)],
+                load_staged_rhs=0 if r == 0 else None,
+            )
+
+        def consume(k, more):
+            src = lax.rem(me + count - k, count)
+            for j in range(chunks):
+                row = piece(src, 0, j).astype(jnp.int32) // cols
+                zero = jnp.zeros((levs, width), jnp.float32)
+                base, nxt, side = zero, zero, zero
+                before = None
+                for r in range(rows):
+                    found = pltpu.matmul_pop(accs[j][r])
+                    if more:
+                        feed(j, r)
+                    if before is not None:
+                        nxt = jnp.where(before, found[:levs], nxt)
+                    if r < rows - 1:
+                        here = jnp.broadcast_to(row == r, (levs, width))
+                        base = jnp.where(here, found[:levs], base)
+                        side = jnp.where(here, found[levs:], side)
+                        before = here
+                level = piece(src, 1, j).astype(jnp.int32)
+                frac = piece(src, 2, j)
+                w0 = piece(src, 3, j)
+                w1 = piece(src, 4, j)
+                column = w0 * base + w1 * nxt + (1.0 - w0 - w1) * side
+                share = jnp.where(lev_iota == level, 1.0 - frac, 0.0)
+                share = jnp.where(lev_iota == level + 1, frac, share)
+                model = jnp.sum(column * share, axis=0, keepdims=True)
+                for t in range(min(2, tiles)):
+                    model_buf[src, pl.ds(j * 2 + t, 1)] = model[:, t * 128 : (t + 1) * 128]
+
+            @pl.when(k > 0)
+            def _():
+                remote(
+                    model_buf.at[src],
+                    model_in.at[me],
+                    model_send.at[src],
+                    model_recv.at[me],
+                    place(src),
+                ).start()
+
+        stage(0)
+        for r in range(rows):
+            for j in range(chunks):
+                feed(j, r)
+
+        def interpolate(k, _):
+            src = lax.rem(me + count - k - 1, count)
             remote(
                 out_buf.at[src], in_buf.at[src], obs_send.at[src], obs_recv.at[src], place(src)
             ).wait_recv()
-
-        for part in range(tiles // group):
-
-            def piece(f):
-                return jnp.concatenate(
-                    [in_buf[src, f, pl.ds(part * group + t, 1)] for t in range(group)], axis=1
-                )
-
-            cell = piece(0).astype(jnp.int32)
-            level = piece(1).astype(jnp.int32)
-            frac = piece(2)
-            w0 = piece(3)
-            w1 = piece(4)
-            w2 = 1.0 - w0 - w1
-            col = cell & (cols - 1)
-            row = cell // cols
-            hot = jnp.where(col_iota == col, 1.0, 0.0).astype(jnp.bfloat16)
-            hot = jnp.concatenate([hot, hot], axis=0)
-            found = jnp.dot(table[...], hot, preferred_element_type=jnp.float32)
-            zero = jnp.zeros((levs, width), jnp.float32)
-            base, nxt, side = zero, zero, zero
-            before = None
-            for r in range(rows):
-                at = r * 2 * levs
-                line = found[at : at + levs]
-                if before is not None:
-                    nxt = jnp.where(before, line, nxt)
-                if r < rows - 1:
-                    here = jnp.broadcast_to(row == r, (levs, width))
-                    base = jnp.where(here, line, base)
-                    side = jnp.where(here, found[at + levs : at + 2 * levs], side)
-                    before = here
-            column = w0 * base + w1 * nxt + w2 * side
-            share = jnp.where(lev_iota == level, 1.0 - frac, 0.0)
-            share = jnp.where(lev_iota == level + 1, frac, share)
-            model = jnp.sum(column * share, axis=0, keepdims=True)
-            for t in range(group):
-                model_buf[src, pl.ds(part * group + t, 1)] = model[:, t * 128 : (t + 1) * 128]
-
-        @pl.when(k > 0)
-        def _():
-            remote(
-                model_buf.at[src],
-                model_in.at[me],
-                model_send.at[src],
-                model_recv.at[me],
-                place(src),
-            ).start()
-
-        return 0
-
-    lax.fori_loop(0, count, interpolate, 0)
+            stage(k + 1)
+            consume(k, True)
+            return 0
+
+        lax.fori_loop(0, count - 1, interpolate, 0)
+        consume(count - 1, False)
+
+    pl.run_scoped(
+        run,
+        [[pltpu.ACC(j)((step_rows, width), jnp.float32) for _ in range(rows)] for j in range(chunks)],
+    )
     model_in[me] = model_buf[me]
 
     def finish(k, _):
@@ -343,6 +412,22 @@
         return 0
 
     lax.fori_loop(0, count // 8, depart, 0)
+    stores[3].start()
+    for store in stores:
+        store.wait()
+
+
+def hand_over(*refs):
+    *pairs, sem = refs
+    half = len(pairs) // 2
+    copies = [
+        pltpu.make_async_copy(src, dst, sem.at[k])
+        for k, (src, dst) in enumerate(zip(pairs[:half], pairs[half:]))
+    ]
+    for copy in copies:
+        copy.start()
+    for copy in copies:
+        copy.wait()
 
 
 def solution(mesh):
@@ -365,16 +450,31 @@
     ):
         levs, rows, cols = theta_field.shape
         tiles = obs_values.shape[2] // 128
-        vmem = pl.BlockSpec(memory_space=pltpu.VMEM)
+        hbm = pl.BlockSpec(memory_space=pltpu.HBM)
         smem = pl.BlockSpec(memory_space=pltpu.SMEM)
         f32 = jnp.float32
+        i32 = jnp.int32
+        bary = jnp.transpose(obs_bary, (0, 2, 1, 3))
         field = jax.ShapeDtypeStruct(theta_field.shape, f32)
-        u_next, v_next, t_next, dep = pl.pallas_call(
+        results = pl.pallas_call(
             functools.partial(kernel, (n_px, n_py, tiles)),
             out_shape=(field, field, field, jax.ShapeDtypeStruct(obs_values.shape, f32)),
-            in_specs=[smem] * 2 + [vmem] * 9,
-            out_specs=[vmem] * 4,
+            in_specs=[smem] * 2 + [hbm] * 9,
+            out_specs=[hbm] * 4,
             scratch_shapes=[
+                pltpu.VMEM(field.shape, f32),
+                pltpu.VMEM(field.shape, f32),
+                pltpu.VMEM(field.shape, f32),
+                pltpu.VMEM(obs_cells.shape, i32),
+                pltpu.VMEM(obs_cells.shape, i32),
+                pltpu.VMEM(bary.shape, f32),
+                pltpu.VMEM(obs_cells.shape, f32),
+                pltpu.VMEM(obs_cells.shape, f32),
+                pltpu.VMEM(obs_cells.shape, i32),
+                pltpu.VMEM(field.shape, f32),
+                pltpu.VMEM(field.shape, f32),
+                pltpu.VMEM(field.shape, f32),
+                pltpu.VMEM(obs_cells.shape, f32),
                 pltpu.VMEM((count, FIELDS, tiles, 128), f32),
                 pltpu.VMEM((count, FIELDS, tiles, 128), f32),
                 pltpu.VMEM((count, tiles, 128), f32),
@@ -391,6 +491,8 @@
                 pltpu.SemaphoreType.DMA((count,)),
                 pltpu.SemaphoreType.DMA((8,)),
                 pltpu.SemaphoreType.DMA((8,)),
+                pltpu.SemaphoreType.DMA((9,)),
+                pltpu.SemaphoreType.DMA((4,)),
             ],
             compiler_params=pltpu.CompilerParams(
                 collective_id=0, has_side_effects=True, vmem_limit_bytes=40 * 1024 * 1024
@@ -403,11 +505,18 @@
             theta_field,
             obs_cells,
             obs_levels,
-            obs_bary,
+            bary,
             obs_vfrac,
             obs_values,
             obs_mask,
         )
+        u_next, v_next, t_next, dep = pl.pallas_call(
+            hand_over,
+            out_shape=[jax.ShapeDtypeStruct(x.shape, x.dtype) for x in results],
+            in_specs=[hbm] * 4,
+            out_specs=[hbm] * 4,
+            scratch_shapes=[pltpu.SemaphoreType.DMA((4,))],
+        )(*results)
         return (t_next, u_next, v_next, dep)
 
     cells = P(None, "px", "py")

time: 51.2 us -> 87.2 us (1.70)
  Pallas kernels: 41.4 us -> 74.7 us
  local copies, waits for them, and re-layouts: 8.76 us -> 11.3 us
    pallas_call x0 -> x1, Pallas kernels: none -> 26.9 us  [on_device(): pl.pallas_call(hand_over, out_shape=[jax.ShapeDtypeStruct(x.shape, x.dtyp...]
    pallas_call x1, Pallas kernels: 41.4 us -> 47.8 us  [on_device(): pl.pallas_call(functools.partial(kernel, (n_px, n_py, tiles)), out_shape=...]
    unnamed x25 -> x30, local copies, waits for them, and re-layouts: 8.76 us -> 11.3 us
where the time goes in v2:
time: 87.2 us; the launch traced here: 86.8 us
  Pallas kernels  74.7 us (86%)
  local copies, waits for them, and re-layouts  11.3 us (13%)
    pallas_call x1, Pallas kernels, on_device(): pl.pallas_call(functools.partial(kernel, (n_px, n_py, tiles)), out_shape=...  47.8 us
    pallas_call x1, Pallas kernels, on_device(): pl.pallas_call(hand_over, out_shape=[jax.ShapeDtypeStruct(x.shape, x.dtyp...  26.9 us
    unnamed x30, local copies, waits for them, and re-layouts  11.3 us

profile of v2, /device:TPU:0, one launch (start us, length us, event | category | flops | bytes accessed | tf_op | source)
XLA Modules:
  0.0 86.8 jit_solution(5293084150535506869)
XLA Ops:
  0.6 0.0 copy-start.14
  0.6 0.0 copy-start.13
  0.7 0.6 copy-done.14
  1.3 0.0 copy-done.13
  1.3 0.0 copy-start.3
  1.3 0.9 %copy-done.3 = f32[32,16,128]{2,1,0:T(8,128)S(1)} copy-done((f32[32,16,128]{2,1,0:T(8,128)S(1)}, f32[32,16,128]{2,1,0:T(8,128)}, u32[]{:S(2)}) %copy-start.3) | copy-done | bytes 262168
  2.3 0.0 copy-start.4
  2.3 0.9 %copy-done.4 = f32[32,16,128]{2,1,0:T(8,128)S(1)} copy-done((f32[32,16,128]{2,1,0:T(8,128)S(1)}, f32[32,16,128]{2,1,0:T(8,128)}, u32[]{:S(2)}) %copy-start.4) | copy-done | bytes 262168
  3.2 0.0 copy-start.5
  3.2 0.9 %copy-done.5 = f32[32,16,128]{2,1,0:T(8,128)S(1)} copy-done((f32[32,16,128]{2,1,0:T(8,128)S(1)}, f32[32,16,128]{2,1,0:T(8,128)}, u32[]{:S(2)}) %copy-start.5) | copy-done | bytes 262168
  4.2 0.0 copy-start.6
  4.2 0.9 %copy-done.6 = f32[1,32,3,512]{3,1,2,0:T(8,128)S(1)} copy-done((f32[1,32,3,512]{3,1,2,0:T(8,128)S(1)}, f32[1,32,3,512]{3,1,2,0:T(8,128)}, u32[]{:S(2)}) %copy-start.6) | copy-done | bytes 196632
  5.1 0.0 copy-start.7
  5.1 0.8 copy-done.7
  5.9 0.0 copy-start.8
  5.9 0.8 copy-done.8
  6.8 0.0 copy-start.9
  6.8 0.8 copy-done.9
  7.6 0.0 copy-start.10
  7.6 0.8 copy-done.10
  8.4 0.0 copy-start.11
  8.4 0.8 copy-done.11
  9.3 47.8 %shard_map.138 = (f32[32,16,128]{2,1,0:T(8,128)S(1)}, f32[32,16,128]{2,1,0:T(8,128)S(1)}, f32[32,16,128]{2,1,0:T(8,128)S(1)}, f32[1,32,512]{2,1,0:T(8,128)S(1)}) custom-call(f32[32]{0:T(128)S(1)} %copy-done.13, f32[32]{0:T(128)S(1)} %copy-done.14, f32[32,16,128]{2,1,0:T(8,128)S(1)} %copy-done.3, f32[32,16,128]{2,1,0:T(8,128)S(1)} %copy-done.4, ...), custom_call_target="tpu_custom_call" | custom-call | tf_op jit(solution)/shard_map/pallas_call | solution.py:459
  57.1 0.0 copy-start
  57.1 0.7 copy-done
  57.8 0.0 copy-start.1
  57.8 0.7 copy-done.1
  58.5 0.0 copy-start.2
  58.5 0.7 copy-done.2
  59.2 0.0 copy-start.12
  59.2 0.6 copy-done.12
  59.8 26.9 %shard_map.139 = (f32[32,16,128]{2,1,0:T(8,128)}, f32[32,16,128]{2,1,0:T(8,128)}, f32[32,16,128]{2,1,0:T(8,128)}, f32[1,32,512]{2,1,0:T(8,128)}) custom-call(f32[32,16,128]{2,1,0:T(8,128)} %copy-done, f32[32,16,128]{2,1,0:T(8,128)} %copy-done.1, f32[32,16,128]{2,1,0:T(8,128)} %copy-done.2, f32[1,32,512]{2,1,0:T(8,128)} %copy-done.12), custom_call_target="tpu_custom_call" | custom-call | tf_op jit(solution)/shard_map/pallas_call | solution.py:513
Async XLA Ops:
  0.6 0.7 copy-start.14
  0.6 0.7 copy-start.13
  1.3 0.9 %copy-start.3 = (f32[32,16,128]{2,1,0:T(8,128)S(1)}, f32[32,16,128]{2,1,0:T(8,128)}, u32[]{:S(2)}) copy-start(f32[32,16,128]{2,1,0:T(8,128)} %u_hbm.1) | copy-start | bytes 786436
  2.3 0.9 %copy-start.4 = (f32[32,16,128]{2,1,0:T(8,128)S(1)}, f32[32,16,128]{2,1,0:T(8,128)}, u32[]{:S(2)}) copy-start(f32[32,16,128]{2,1,0:T(8,128)} %v_hbm.1) | copy-start | bytes 786436
  3.2 0.9 %copy-start.5 = (f32[32,16,128]{2,1,0:T(8,128)S(1)}, f32[32,16,128]{2,1,0:T(8,128)}, u32[]{:S(2)}) copy-start(f32[32,16,128]{2,1,0:T(8,128)} %t_hbm.1) | copy-start | bytes 786436
  4.2 0.9 %copy-start.6 = (f32[1,32,3,512]{3,1,2,0:T(8,128)S(1)}, f32[1,32,3,512]{3,1,2,0:T(8,128)}, u32[]{:S(2)}) copy-start(f32[1,32,3,512]{3,1,2,0:T(8,128)} %param.18) | copy-start | bytes 589828
  5.1 0.8 copy-start.7
  5.9 0.8 copy-start.8
  6.8 0.8 copy-start.9
  7.6 0.8 copy-start.10
  8.4 0.8 copy-start.11
  57.1 0.7 copy-start
  57.8 0.7 copy-start.1
  58.5 0.7 copy-start.2
  59.2 0.6 copy-start.12

commit v3 on v1

--- a/solution.py
+++ b/solution.py
@@ -37,6 +37,19 @@
     sizes,
     hyper,
     damp,
+    u_hbm,
+    v_hbm,
+    t_hbm,
+    cells_hbm,
+    levels_hbm,
+    bary_hbm,
+    vfrac_hbm,
+    values_hbm,
+    mask_hbm,
+    u_out,
+    v_out,
+    t_out,
+    dep_out,
     u_ref,
     v_ref,
     t_ref,
@@ -46,10 +59,6 @@
     vfrac_ref,
     values_ref,
     mask_ref,
-    u_out,
-    v_out,
-    t_out,
-    dep_out,
     out_buf,
     in_buf,
     model_buf,
@@ -66,6 +75,7 @@
     model_recv,
     halo_send,
     halo_recv,
+    load_sem,
 ):
     n_px, n_py, tiles = sizes
     count = n_px * n_py
@@ -78,6 +88,25 @@
     def place(dev):
         return (dev // n_py, dev % n_py)
 
+    loads = [
+        pltpu.make_async_copy(src, dst, load_sem.at[k])
+        for k, (src, dst) in enumerate(
+            (
+                (u_hbm, u_ref),
+                (v_hbm, v_ref),
+                (t_hbm, t_ref),
+                (cells_hbm, cells_ref),
+                (levels_hbm, levels_ref),
+                (vfrac_hbm, vfrac_ref),
+                (bary_hbm, bary_ref),
+                (values_hbm, values_ref),
+                (mask_hbm, mask_ref),
+            )
+        )
+    ]
+    for load in loads:
+        load.start()
+
     barrier = pltpu.get_barrier_semaphore()
 
     def greet(k, _):
@@ -91,6 +120,9 @@
     row8 = lax.broadcasted_iota(jnp.int32, (8, cols), 0)
     lane16 = lax.broadcasted_iota(jnp.int32, (rows, cols), 1)
     lane24 = lax.broadcasted_iota(jnp.int32, (rows + 8, cols), 1)
+
+    for load in loads[:3]:
+        load.wait()
 
     def pack_edges(g, _):
         edge = jnp.zeros((rows, cols), jnp.float32)
@@ -121,6 +153,9 @@
 
     lax.fori_loop(0, levs // 8, pack_edges, 0)
 
+    for load in loads[3:]:
+        load.wait()
+
     def pack_obs(g, _):
         lines = pl.ds(pl.multiple_of(g * 8, 8), 8)
         for t in range(tiles):
@@ -129,12 +164,12 @@
                 cells_ref[0, lines, part].astype(jnp.float32),
                 levels_ref[0, lines, part].astype(jnp.float32),
                 vfrac_ref[0, lines, part],
+                bary_ref[0, 0, lines, part],
+                bary_ref[0, 1, lines, part],
             )
             for i in range(8):
                 for f, x in enumerate(whole):
                     out_buf[g * 8 + i, f, pl.ds(t, 1)] = x[i : i + 1]
-                for j in range(2):
-                    out_buf[g * 8 + i, 3 + j, pl.ds(t, 1)] = bary_ref[0, g * 8 + i, pl.ds(j, 1), part]
         return 0
 
     lax.fori_loop(0, count // 8, pack_obs, 0)
@@ -238,20 +273,12 @@
     lax.fori_loop(0, levs // 4, advance, 0)
 
     for r in range(rows):
-        line = t_out[:, r, :]
-        for step in range(2):
-            if step:
-                line = pltpu.roll(line, cols - 1, 1)
-            high = line.astype(jnp.bfloat16)
-            low = (line - high.astype(jnp.float32)).astype(jnp.bfloat16)
-            at = (r * 2 + step) * levs
-            table[pl.ds(at, levs), pl.ds(0, cols)] = high
-            table[pl.ds(at, levs), pl.ds(cols, cols)] = low
-
-    group = 2 if tiles % 2 == 0 else 1
-    width = group * 128
-    col_iota = lax.broadcasted_iota(jnp.int32, (cols, width), 0)
-    lev_iota = lax.broadcasted_iota(jnp.int32, (levs, width), 0)
+        table[pl.ds(r * levs, levs)] = t_out[:, r, :]
+
+    lev_iota = lax.broadcasted_iota(jnp.int32, (levs, 128), 0)
+
+    def pick(x, index):
+        return jnp.take_along_axis(x, index, axis=1, mode="promise_in_bounds")
 
     def interpolate(k, _):
         src = lax.rem(me + count - k, count)
@@ -262,43 +289,38 @@
                 out_buf.at[src], in_buf.at[src], obs_send.at[src], obs_recv.at[src], place(src)
             ).wait_recv()
 
-        for part in range(tiles // group):
+        for t in range(tiles):
 
             def piece(f):
-                return jnp.concatenate(
-                    [in_buf[src, f, pl.ds(part * group + t, 1)] for t in range(group)], axis=1
-                )
+                return in_buf[src, f, pl.ds(t, 1)]
 
             cell = piece(0).astype(jnp.int32)
+            row = jnp.broadcast_to(cell // cols, (8, 128))
+            col = jnp.broadcast_to(cell & (cols - 1), (8, 128))
+            col_next = col + 1
+            zero = jnp.zeros((8, 128), jnp.float32)
+            base, nxt, side = ([zero] * (levs // 8) for _ in range(3))
+            before = None
+            for r in range(rows):
+                here = row == r
+                for part in range(levs // 8):
+                    line = table[pl.ds(r * levs + part * 8, 8)]
+                    found = pick(line, col)
+                    if before is not None:
+                        nxt[part] = jnp.where(before, found, nxt[part])
+                    if r < rows - 1:
+                        base[part] = jnp.where(here, found, base[part])
+                        side[part] = jnp.where(here, pick(line, col_next), side[part])
+                before = here
+            base, nxt, side = (jnp.concatenate(x, axis=0) for x in (base, nxt, side))
             level = piece(1).astype(jnp.int32)
             frac = piece(2)
             w0 = piece(3)
             w1 = piece(4)
-            w2 = 1.0 - w0 - w1
-            col = cell & (cols - 1)
-            row = cell // cols
-            hot = jnp.where(col_iota == col, 1.0, 0.0).astype(jnp.bfloat16)
-            hot = jnp.concatenate([hot, hot], axis=0)
-            found = jnp.dot(table[...], hot, preferred_element_type=jnp.float32)
-            zero = jnp.zeros((levs, width), jnp.float32)
-            base, nxt, side = zero, zero, zero
-            before = None
-            for r in range(rows):
-                at = r * 2 * levs
-                line = found[at : at + levs]
-                if before is not None:
-                    nxt = jnp.where(before, line, nxt)
-                if r < rows - 1:
-                    here = jnp.broadcast_to(row == r, (levs, width))
-                    base = jnp.where(here, line, base)
-                    side = jnp.where(here, found[at + levs : at + 2 * levs], side)
-                    before = here
-            column = w0 * base + w1 * nxt + w2 * side
+            column = w0 * base + w1 * nxt + (1.0 - w0 - w1) * side
             share = jnp.where(lev_iota == level, 1.0 - frac, 0.0)
             share = jnp.where(lev_iota == level + 1, frac, share)
-            model = jnp.sum(column * share, axis=0, keepdims=True)
-            for t in range(group):
-                model_buf[src, pl.ds(part * group + t, 1)] = model[:, t * 128 : (t + 1) * 128]
+            model_buf[src, pl.ds(t, 1)] = jnp.sum(column * share, axis=0, keepdims=True)
 
         @pl.when(k > 0)
         def _():
@@ -343,6 +365,19 @@
         return 0
 
     lax.fori_loop(0, count // 8, depart, 0)
+
+
+def hand_over(*refs):
+    *pairs, sem = refs
+    half = len(pairs) // 2
+    copies = [
+        pltpu.make_async_copy(src, dst, sem.at[k])
+        for k, (src, dst) in enumerate(zip(pairs[:half], pairs[half:]))
+    ]
+    for copy in copies:
+        copy.start()
+    for copy in copies:
+        copy.wait()
 
 
 def solution(mesh):
@@ -365,16 +400,28 @@
     ):
         levs, rows, cols = theta_field.shape
         tiles = obs_values.shape[2] // 128
+        hbm = pl.BlockSpec(memory_space=pltpu.HBM)
         vmem = pl.BlockSpec(memory_space=pltpu.VMEM)
         smem = pl.BlockSpec(memory_space=pltpu.SMEM)
         f32 = jnp.float32
+        i32 = jnp.int32
+        bary = jnp.transpose(obs_bary, (0, 2, 1, 3))
         field = jax.ShapeDtypeStruct(theta_field.shape, f32)
-        u_next, v_next, t_next, dep = pl.pallas_call(
+        results = pl.pallas_call(
             functools.partial(kernel, (n_px, n_py, tiles)),
             out_shape=(field, field, field, jax.ShapeDtypeStruct(obs_values.shape, f32)),
-            in_specs=[smem] * 2 + [vmem] * 9,
+            in_specs=[smem] * 2 + [hbm] * 9,
             out_specs=[vmem] * 4,
             scratch_shapes=[
+                pltpu.VMEM(field.shape, f32),
+                pltpu.VMEM(field.shape, f32),
+                pltpu.VMEM(field.shape, f32),
+                pltpu.VMEM(obs_cells.shape, i32),
+                pltpu.VMEM(obs_cells.shape, i32),
+                pltpu.VMEM(bary.shape, f32),
+                pltpu.VMEM(obs_cells.shape, f32),
+                pltpu.VMEM(obs_cells.shape, f32),
+                pltpu.VMEM(obs_cells.shape, i32),
                 pltpu.VMEM((count, FIELDS, tiles, 128), f32),
                 pltpu.VMEM((count, FIELDS, tiles, 128), f32),
                 pltpu.VMEM((count, tiles, 128), f32),
@@ -384,17 +431,16 @@
                 pltpu.VMEM((levs // 8, rows, cols), f32),
                 pltpu.VMEM((2, levs // 8, rows, cols), f32),
                 pltpu.VMEM((4, levs // 8, 8, cols), f32),
-                pltpu.VMEM((rows * 2 * levs, 2 * cols), jnp.bfloat16),
+                pltpu.VMEM((rows * levs, cols), f32),
                 pltpu.SemaphoreType.DMA((count,)),
                 pltpu.SemaphoreType.DMA((count,)),
                 pltpu.SemaphoreType.DMA((count,)),
                 pltpu.SemaphoreType.DMA((count,)),
                 pltpu.SemaphoreType.DMA((8,)),
                 pltpu.SemaphoreType.DMA((8,)),
+                pltpu.SemaphoreType.DMA((9,)),
             ],
-            compiler_params=pltpu.CompilerParams(
-                collective_id=0, has_side_effects=True, vmem_limit_bytes=40 * 1024 * 1024
-            ),
+            compiler_params=pltpu.CompilerParams(collective_id=0, has_side_effects=True),
         )(
             hyper_coef,
             damp_coef,
@@ -403,11 +449,18 @@
             theta_field,
             obs_cells,
             obs_levels,
-            obs_bary,
+            bary,
             obs_vfrac,
             obs_values,
             obs_mask,
         )
+        u_next, v_next, t_next, dep = pl.pallas_call(
+            hand_over,
+            out_shape=[jax.ShapeDtypeStruct(x.shape, x.dtype) for x in results],
+            in_specs=[vmem] * 4,
+            out_specs=[hbm] * 4,
+            scratch_shapes=[pltpu.SemaphoreType.DMA((4,))],
+        )(*results)
         return (t_next, u_next, v_next, dep)
 
     cells = P(None, "px", "py")

time: 51.2 us -> 61.7 us (1.21)
  Pallas kernels: 41.4 us -> 60.9 us
  local copies, waits for them, and re-layouts: 8.76 us -> 0 us
    pallas_call x1, Pallas kernels: 41.4 us -> 58.8 us  [on_device(): pl.pallas_call(functools.partial(kernel, (n_px, n_py, tiles)), out_shape=...]
    unnamed x25 -> x0, local copies, waits for them, and re-layouts: 8.76 us -> none
    pallas_call x0 -> x1, Pallas kernels: none -> 2.03 us  [on_device(): pl.pallas_call(hand_over, out_shape=[jax.ShapeDtypeStruct(x.shape, x.dtyp...]
where the time goes in v3:
time: 61.7 us; the launch traced here: 61.5 us
  Pallas kernels  60.9 us (99%)
  between operations  0.64 us (1%)
    pallas_call x1, Pallas kernels, on_device(): pl.pallas_call(functools.partial(kernel, (n_px, n_py, tiles)), out_shape=...  58.8 us
    pallas_call x1, Pallas kernels, on_device(): pl.pallas_call(hand_over, out_shape=[jax.ShapeDtypeStruct(x.shape, x.dtyp...  2.03 us

profile of v3, /device:TPU:0, one launch (start us, length us, event | category | flops | bytes accessed | tf_op | source)
XLA Modules:
  0.0 61.5 jit_solution(7882107393997343150)
XLA Ops:
  0.6 58.8 %shard_map.138 = (f32[32,16,128]{2,1,0:T(8,128)}, f32[32,16,128]{2,1,0:T(8,128)}, f32[32,16,128]{2,1,0:T(8,128)}, f32[1,32,512]{2,1,0:T(8,128)}) custom-call(f32[32]{0:T(128)} %hyper.1, f32[32]{0:T(128)} %damp.1, f32[32,16,128]{2,1,0:T(8,128)} %u_hbm.1, f32[32,16,128]{2,1,0:T(8,128)} %v_hbm.1, f32[32,16,128]{2,1,0:T(8,128)} %t_hbm.1, ...), custom_call_target="tpu_custom_call" | custom-call | tf_op jit(solution)/shard_map/pallas_call | solution.py:410
  59.5 2.0 %shard_map.139 = (f32[32,16,128]{2,1,0:T(8,128)}, f32[32,16,128]{2,1,0:T(8,128)}, f32[32,16,128]{2,1,0:T(8,128)}, f32[1,32,512]{2,1,0:T(8,128)}) custom-call(f32[32,16,128]{2,1,0:T(8,128)} %get-tuple-element.12.refs_0_, f32[32,16,128]{2,1,0:T(8,128)} %get-tuple-element.13.refs_1_, f32[32,16,128]{2,1,0:T(8,128)} %get-tuple-element.14.refs_2_, ...), custom_call_target="tpu_custom_call" | custom-call | tf_op jit(solution)/shard_map/pallas_call | solution.py:457

commit v4 on v2

--- a/solution.py
+++ b/solution.py
@@ -46,10 +46,10 @@
     vfrac_hbm,
     values_hbm,
     mask_hbm,
-    u_res,
-    v_res,
-    t_res,
-    dep_res,
+    u_out,
+    v_out,
+    t_out,
+    dep_out,
     u_ref,
     v_ref,
     t_ref,
@@ -59,10 +59,6 @@
     vfrac_ref,
     values_ref,
     mask_ref,
-    u_out,
-    v_out,
-    t_out,
-    dep_out,
     out_buf,
     in_buf,
     model_buf,
@@ -80,7 +76,6 @@
     halo_send,
     halo_recv,
     load_sem,
-    store_sem,
 ):
     n_px, n_py, tiles = sizes
     count = n_px * n_py
@@ -276,14 +271,6 @@
         return 0
 
     lax.fori_loop(0, levs // 4, advance, 0)
-    stores = [
-        pltpu.make_async_copy(src, dst, store_sem.at[k])
-        for k, (src, dst) in enumerate(
-            ((u_out, u_res), (v_out, v_res), (t_out, t_res), (dep_out, dep_res))
-        )
-    ]
-    for store in stores[:3]:
-        store.start()
 
     for r in range(rows):
         line = t_out[:, r, :]
@@ -298,9 +285,9 @@
 
     chunks = max(1, tiles // 2)
     width = 256
-    step_rows = 2 * levs
     col_iota = lax.broadcasted_iota(jnp.int32, (cols, width), 0)
     lev_iota = lax.broadcasted_iota(jnp.int32, (levs, width), 0)
+    pieces = [(r, step) for r in range(rows) for step in range(2) if r < rows - 1 or not step]
 
     def piece(src, f, j):
         return jnp.concatenate(
@@ -315,36 +302,41 @@
             pltpu.matmul_push_rhs(jnp.concatenate([hot, hot], axis=0), 0, j)
 
     def run(accs):
-        def feed(j, r):
+        def feed(j, p):
+            r, step = pieces[p]
             pltpu.matmul_acc_lhs(
-                accs[j][r],
-                table[pl.ds(r * step_rows, step_rows)],
-                load_staged_rhs=0 if r == 0 else None,
+                accs[j][p],
+                table[pl.ds((r * 2 + step) * levs, levs)],
+                load_staged_rhs=0 if p == 0 else None,
             )
 
         def consume(k, more):
             src = lax.rem(me + count - k, count)
+            zero = jnp.zeros((levs, width), jnp.float32)
+            base, nxt, side = ([zero] * chunks for _ in range(3))
+            row = [piece(src, 0, j).astype(jnp.int32) // cols for j in range(chunks)]
+            before = [None] * chunks
+            here = [None] * chunks
+            for p, (r, step) in enumerate(pieces):
+                for j in range(chunks):
+                    found = pltpu.matmul_pop(accs[j][p])
+                    if more:
+                        feed(j, p)
+                    if step:
+                        side[j] = jnp.where(here[j], found, side[j])
+                        continue
+                    before[j] = here[j]
+                    if r:
+                        nxt[j] = jnp.where(before[j], found, nxt[j])
+                    if r < rows - 1:
+                        here[j] = jnp.broadcast_to(row[j] == r, (levs, width))
+                        base[j] = jnp.where(here[j], found, base[j])
             for j in range(chunks):
-                row = piece(src, 0, j).astype(jnp.int32) // cols
-                zero = jnp.zeros((levs, width), jnp.float32)
-                base, nxt, side = zero, zero, zero
-                before = None
-                for r in range(rows):
-                    found = pltpu.matmul_pop(accs[j][r])
-                    if more:
-                        feed(j, r)
-                    if before is not None:
-                        nxt = jnp.where(before, found[:levs], nxt)
-                    if r < rows - 1:
-                        here = jnp.broadcast_to(row == r, (levs, width))
-                        base = jnp.where(here, found[:levs], base)
-                        side = jnp.where(here, found[levs:], side)
-                        before = here
                 level = piece(src, 1, j).astype(jnp.int32)
                 frac = piece(src, 2, j)
                 w0 = piece(src, 3, j)
                 w1 = piece(src, 4, j)
-                column = w0 * base + w1 * nxt + (1.0 - w0 - w1) * side
+                column = w0 * base[j] + w1 * nxt[j] + (1.0 - w0 - w1) * side[j]
                 share = jnp.where(lev_iota == level, 1.0 - frac, 0.0)
                 share = jnp.where(lev_iota == level + 1, frac, share)
                 model = jnp.sum(column * share, axis=0, keepdims=True)
@@ -362,9 +354,9 @@
                 ).start()
 
         stage(0)
-        for r in range(rows):
+        for p in range(len(pieces)):
             for j in range(chunks):
-                feed(j, r)
+                feed(j, p)
 
         def interpolate(k, _):
             src = lax.rem(me + count - k - 1, count)
@@ -380,7 +372,7 @@
 
     pl.run_scoped(
         run,
-        [[pltpu.ACC(j)((step_rows, width), jnp.float32) for _ in range(rows)] for j in range(chunks)],
+        [[pltpu.ACC(j)((levs, width), jnp.float32) for _ in pieces] for j in range(chunks)],
     )
     model_in[me] = model_buf[me]
 
@@ -412,9 +404,6 @@
         return 0
 
     lax.fori_loop(0, count // 8, depart, 0)
-    stores[3].start()
-    for store in stores:
-        store.wait()
 
 
 def hand_over(*refs):
@@ -451,6 +440,7 @@
         levs, rows, cols = theta_field.shape
         tiles = obs_values.shape[2] // 128
         hbm = pl.BlockSpec(memory_space=pltpu.HBM)
+        vmem = pl.BlockSpec(memory_space=pltpu.VMEM)
         smem = pl.BlockSpec(memory_space=pltpu.SMEM)
         f32 = jnp.float32
         i32 = jnp.int32
@@ -460,7 +450,7 @@
             functools.partial(kernel, (n_px, n_py, tiles)),
             out_shape=(field, field, field, jax.ShapeDtypeStruct(obs_values.shape, f32)),
             in_specs=[smem] * 2 + [hbm] * 9,
-            out_specs=[hbm] * 4,
+            out_specs=[vmem] * 4,
             scratch_shapes=[
                 pltpu.VMEM(field.shape, f32),
                 pltpu.VMEM(field.shape, f32),
@@ -471,10 +461,6 @@
                 pltpu.VMEM(obs_cells.shape, f32),
                 pltpu.VMEM(obs_cells.shape, f32),
                 pltpu.VMEM(obs_cells.shape, i32),
-                pltpu.VMEM(field.shape, f32),
-                pltpu.VMEM(field.shape, f32),
-                pltpu.VMEM(field.shape, f32),
-                pltpu.VMEM(obs_cells.shape, f32),
                 pltpu.VMEM((count, FIELDS, tiles, 128), f32),
                 pltpu.VMEM((count, FIELDS, tiles, 128), f32),
                 pltpu.VMEM((count, tiles, 128), f32),
@@ -492,11 +478,8 @@
                 pltpu.SemaphoreType.DMA((8,)),
                 pltpu.SemaphoreType.DMA((8,)),
                 pltpu.SemaphoreType.DMA((9,)),
-                pltpu.SemaphoreType.DMA((4,)),
             ],
-            compiler_params=pltpu.CompilerParams(
-                collective_id=0, has_side_effects=True, vmem_limit_bytes=40 * 1024 * 1024
-            ),
+            compiler_params=pltpu.CompilerParams(collective_id=0, has_side_effects=True),
         )(
             hyper_coef,
             damp_coef,
@@ -513,7 +496,7 @@
         u_next, v_next, t_next, dep = pl.pallas_call(
             hand_over,
             out_shape=[jax.ShapeDtypeStruct(x.shape, x.dtype) for x in results],
-            in_specs=[hbm] * 4,
+            in_specs=[vmem] * 4,
             out_specs=[hbm] * 4,
             scratch_shapes=[pltpu.SemaphoreType.DMA((4,))],
         )(*results)

time: 87.2 us -> 50.4 us (0.58)
  Pallas kernels: 74.7 us -> 49.6 us
  local copies, waits for them, and re-layouts: 11.3 us -> 0 us
    pallas_call x1, Pallas kernels: 26.9 us -> 2.03 us  [on_device(): pl.pallas_call(hand_over, out_shape=[jax.ShapeDtypeStruct(x.shape, x.dtyp...]
    unnamed x30 -> x0, local copies, waits for them, and re-layouts: 11.3 us -> none
where the time goes in v4:
time: 50.4 us; the launch traced here: 50.2 us
  Pallas kernels  49.6 us (98%)
  between operations  0.64 us (1%)
    pallas_call x1, Pallas kernels, on_device(): pl.pallas_call(functools.partial(kernel, (n_px, n_py, tiles)), out_shape=...  47.6 us
    pallas_call x1, Pallas kernels, on_device(): pl.pallas_call(hand_over, out_shape=[jax.ShapeDtypeStruct(x.shape, x.dtyp...  2.03 us

profile of v4, /device:TPU:0, one launch (start us, length us, event | category | flops | bytes accessed | tf_op | source)
XLA Modules:
  0.0 50.2 jit_solution(6371628938644204941)
XLA Ops:
  0.6 47.6 %shard_map.138 = (f32[32,16,128]{2,1,0:T(8,128)}, f32[32,16,128]{2,1,0:T(8,128)}, f32[32,16,128]{2,1,0:T(8,128)}, f32[1,32,512]{2,1,0:T(8,128)}) custom-call(f32[32]{0:T(128)} %hyper.1, f32[32]{0:T(128)} %damp.1, f32[32,16,128]{2,1,0:T(8,128)} %u_hbm.1, f32[32,16,128]{2,1,0:T(8,128)} %v_hbm.1, f32[32,16,128]{2,1,0:T(8,128)} %t_hbm.1, ...), custom_call_target="tpu_custom_call" | custom-call | tf_op jit(solution)/shard_map/pallas_call | solution.py:449
  48.2 2.0 %shard_map.139 = (f32[32,16,128]{2,1,0:T(8,128)}, f32[32,16,128]{2,1,0:T(8,128)}, f32[32,16,128]{2,1,0:T(8,128)}, f32[1,32,512]{2,1,0:T(8,128)}) custom-call(f32[32,16,128]{2,1,0:T(8,128)} %get-tuple-element.12.refs_0_, f32[32,16,128]{2,1,0:T(8,128)} %get-tuple-element.13.refs_1_, f32[32,16,128]{2,1,0:T(8,128)} %get-tuple-element.14.refs_2_, ...), custom_call_target="tpu_custom_call" | custom-call | tf_op jit(solution)/shard_map/pallas_call | solution.py:496

commit v5 on v3

--- a/solution.py
+++ b/solution.py
@@ -273,12 +273,24 @@
     lax.fori_loop(0, levs // 4, advance, 0)
 
     for r in range(rows):
-        table[pl.ds(r * levs, levs)] = t_out[:, r, :]
-
-    lev_iota = lax.broadcasted_iota(jnp.int32, (levs, 128), 0)
-
-    def pick(x, index):
-        return jnp.take_along_axis(x, index, axis=1, mode="promise_in_bounds")
+        line = t_out[:, r, :]
+        for step in range(2):
+            if step:
+                line = pltpu.roll(line, cols - 1, 1)
+            high = line.astype(jnp.bfloat16)
+            low = (line - high.astype(jnp.float32)).astype(jnp.bfloat16)
+            at = (r * 2 + step) * levs
+            table[pl.ds(at, levs), pl.ds(0, cols)] = high
+            table[pl.ds(at, levs), pl.ds(cols, cols)] = low
+
+    chunks = max(1, tiles // 2)
+    width = 256
+    col_iota = lax.broadcasted_iota(jnp.int32, (cols, width), 0)
+    lev_iota = lax.broadcasted_iota(jnp.int32, (levs, width), 0)
+    def piece(src, f, j):
+        return jnp.concatenate(
+            [in_buf[src, f, pl.ds(min(j * 2 + t, tiles - 1), 1)] for t in range(2)], axis=1
+        )
 
     def interpolate(k, _):
         src = lax.rem(me + count - k, count)
@@ -289,38 +301,35 @@
                 out_buf.at[src], in_buf.at[src], obs_send.at[src], obs_recv.at[src], place(src)
             ).wait_recv()
 
-        for t in range(tiles):
-
-            def piece(f):
-                return in_buf[src, f, pl.ds(t, 1)]
-
-            cell = piece(0).astype(jnp.int32)
-            row = jnp.broadcast_to(cell // cols, (8, 128))
-            col = jnp.broadcast_to(cell & (cols - 1), (8, 128))
-            col_next = col + 1
-            zero = jnp.zeros((8, 128), jnp.float32)
-            base, nxt, side = ([zero] * (levs // 8) for _ in range(3))
+        for j in range(chunks):
+            cell = piece(src, 0, j).astype(jnp.int32)
+            row = cell // cols
+            hot = jnp.where(col_iota == (cell & (cols - 1)), 1.0, 0.0).astype(jnp.bfloat16)
+            hot = jnp.concatenate([hot, hot], axis=0)
+            found = jnp.dot(table[...], hot, preferred_element_type=jnp.float32)
+            zero = jnp.zeros((levs, width), jnp.float32)
+            base, nxt, side = zero, zero, zero
             before = None
             for r in range(rows):
-                here = row == r
-                for part in range(levs // 8):
-                    line = table[pl.ds(r * levs + part * 8, 8)]
-                    found = pick(line, col)
-                    if before is not None:
-                        nxt[part] = jnp.where(before, found, nxt[part])
-                    if r < rows - 1:
-                        base[part] = jnp.where(here, found, base[part])
-                        side[part] = jnp.where(here, pick(line, col_next), side[part])
-                before = here
-            base, nxt, side = (jnp.concatenate(x, axis=0) for x in (base, nxt, side))
-            level = piece(1).astype(jnp.int32)
-            frac = piece(2)
-            w0 = piece(3)
-            w1 = piece(4)
+                at = r * 2 * levs
+                line = found[at : at + levs]
+                if before is not None:
+                    nxt = jnp.where(before, line, nxt)
+                if r < rows - 1:
+                    here = jnp.broadcast_to(row == r, (levs, width))
+                    base = jnp.where(here, line, base)
+                    side = jnp.where(here, found[at + levs : at + 2 * levs], side)
+                    before = here
+            level = piece(src, 1, j).astype(jnp.int32)
+            frac = piece(src, 2, j)
+            w0 = piece(src, 3, j)
+            w1 = piece(src, 4, j)
             column = w0 * base + w1 * nxt + (1.0 - w0 - w1) * side
             share = jnp.where(lev_iota == level, 1.0 - frac, 0.0)
             share = jnp.where(lev_iota == level + 1, frac, share)
-            model_buf[src, pl.ds(t, 1)] = jnp.sum(column * share, axis=0, keepdims=True)
+            model = jnp.sum(column * share, axis=0, keepdims=True)
+            for t in range(min(2, tiles)):
+                model_buf[src, pl.ds(j * 2 + t, 1)] = model[:, t * 128 : (t + 1) * 128]
 
         @pl.when(k > 0)
         def _():
@@ -431,7 +440,7 @@
                 pltpu.VMEM((levs // 8, rows, cols), f32),
                 pltpu.VMEM((2, levs // 8, rows, cols), f32),
                 pltpu.VMEM((4, levs // 8, 8, cols), f32),
-                pltpu.VMEM((rows * levs, cols), f32),
+                pltpu.VMEM((rows * 2 * levs, 2 * cols), jnp.bfloat16),
                 pltpu.SemaphoreType.DMA((count,)),
                 pltpu.SemaphoreType.DMA((count,)),
                 pltpu.SemaphoreType.DMA((count,)),

time: 61.7 us -> 45.4 us (0.74)
  Pallas kernels: 60.9 us -> 44.6 us
    pallas_call x1, Pallas kernels: 58.8 us -> 42.5 us  [on_device(): pl.pallas_call(functools.partial(kernel, (n_px, n_py, tiles)), out_shape=...]
where the time goes in v5:
time: 45.4 us; the launch traced here: 45.2 us
  Pallas kernels  44.6 us (98%)
  between operations  0.64 us (1%)
    pallas_call x1, Pallas kernels, on_device(): pl.pallas_call(functools.partial(kernel, (n_px, n_py, tiles)), out_shape=...  42.5 us
    pallas_call x1, Pallas kernels, on_device(): pl.pallas_call(hand_over, out_shape=[jax.ShapeDtypeStruct(x.shape, x.dtyp...  2.03 us

profile of v5, /device:TPU:0, one launch (start us, length us, event | category | flops | bytes accessed | tf_op | source)
XLA Modules:
  0.0 45.2 jit_solution(14689707438634878108)
XLA Ops:
  0.6 42.5 %shard_map.138 = (f32[32,16,128]{2,1,0:T(8,128)}, f32[32,16,128]{2,1,0:T(8,128)}, f32[32,16,128]{2,1,0:T(8,128)}, f32[1,32,512]{2,1,0:T(8,128)}) custom-call(f32[32]{0:T(128)} %hyper.1, f32[32]{0:T(128)} %damp.1, f32[32,16,128]{2,1,0:T(8,128)} %u_hbm.1, f32[32,16,128]{2,1,0:T(8,128)} %v_hbm.1, f32[32,16,128]{2,1,0:T(8,128)} %t_hbm.1, ...), custom_call_target="tpu_custom_call" | custom-call | tf_op jit(solution)/shard_map/pallas_call | solution.py:419
  43.2 2.0 %shard_map.139 = (f32[32,16,128]{2,1,0:T(8,128)}, f32[32,16,128]{2,1,0:T(8,128)}, f32[32,16,128]{2,1,0:T(8,128)}, f32[1,32,512]{2,1,0:T(8,128)}) custom-call(f32[32,16,128]{2,1,0:T(8,128)} %get-tuple-element.12.refs_0_, f32[32,16,128]{2,1,0:T(8,128)} %get-tuple-element.13.refs_1_, f32[32,16,128]{2,1,0:T(8,128)} %get-tuple-element.14.refs_2_, ...), custom_call_target="tpu_custom_call" | custom-call | tf_op jit(solution)/shard_map/pallas_call | solution.py:466

commit v6 on v5

--- a/solution.py
+++ b/solution.py
@@ -12,25 +12,32 @@
 CORNERS = ((-1, -1), (-1, 1), (1, -1), (1, 1))
 
 
-def laplace(x):
-    rows, cols = x.shape
-    below = pltpu.roll(x, rows - 1, 0)
-    above = pltpu.roll(x, 1, 0)
+def east(lane, main, side):
+    last = main.shape[1] - 1
     return (
-        below
-        + above
-        + pltpu.roll(x + above, cols - 1, 1)
-        + pltpu.roll(x + below, 1, 1)
-        - 6.0 * x
+        pltpu.roll(jnp.where(lane == 0, side, main), last, 1),
+        pltpu.roll(jnp.where(lane == 0, main, side), last, 1),
     )
 
 
-def diff_x(x):
-    return (pltpu.roll(x, x.shape[0] - 1, 0) - pltpu.roll(x, 1, 0)) * 0.5
-
-
-def diff_y(x):
-    return (pltpu.roll(x, x.shape[1] - 1, 1) - pltpu.roll(x, 1, 1)) * 0.5
+def west(lane, main, side):
+    last = main.shape[1] - 1
+    return (
+        pltpu.roll(jnp.where(lane == last, side, main), 1, 1),
+        pltpu.roll(jnp.where(lane == last, main, side), 1, 1),
+    )
+
+
+def laplace(lane, above, mid, below):
+    right = east(lane, mid[0] + above[0], mid[1] + above[1])
+    left = west(lane, mid[0] + below[0], mid[1] + below[1])
+    return [below[k] + above[k] + right[k] + left[k] - 6.0 * mid[k] for k in range(2)]
+
+
+def diff_y(lane, mid):
+    right = east(lane, *mid)
+    left = west(lane, *mid)
+    return [(right[k] - left[k]) * 0.5 for k in range(2)]
 
 
 def kernel(
@@ -63,8 +70,11 @@
     in_buf,
     model_buf,
     model_in,
-    row_buf,
-    row_in,
+    coefs,
+    main,
+    side,
+    lap_main,
+    lap_side,
     col_buf,
     col_in,
     corner_in,
@@ -117,41 +127,22 @@
 
     lax.fori_loop(1, count, greet, 0)
 
-    row8 = lax.broadcasted_iota(jnp.int32, (8, cols), 0)
-    lane16 = lax.broadcasted_iota(jnp.int32, (rows, cols), 1)
-    lane24 = lax.broadcasted_iota(jnp.int32, (rows + 8, cols), 1)
-
+    lane = lax.broadcasted_iota(jnp.int32, (levs, cols), 1)
+    for l in range(levs):
+        coefs[0, pl.ds(l, 1)] = jnp.full((1, cols), hyper[l], jnp.float32)
+        coefs[1, pl.ds(l, 1)] = jnp.full((1, cols), damp[l], jnp.float32)
     for load in loads[:3]:
         load.wait()
 
-    def pack_edges(g, _):
-        edge = jnp.zeros((rows, cols), jnp.float32)
-        for f, ref in enumerate(fields):
-            for half in range(2):
-                top = jnp.zeros((8, cols), jnp.float32)
-                bottom = top
-                for i in range(4):
-                    at = half * 4 + i
-                    x = ref[g * 8 + at]
-                    base = 16 * at + 4 * f
-                    edge = jnp.where(
-                        lane16 // 4 == base // 4, pltpu.roll(x, (base + 2) % cols, 1), edge
-                    )
-                    here = row8 // 2 == i
-                    head = x[:8]
-                    tail = x[rows - 8 :]
-                    if i:
-                        head = pltpu.roll(head, 2 * i, 0)
-                    if (2 * i + 2) % 8:
-                        tail = pltpu.roll(tail, 2 * i + 2, 0)
-                    top = jnp.where(here, head, top)
-                    bottom = jnp.where(here, tail, bottom)
-                row_buf[0, f, g * 2 + half] = top
-                row_buf[1, f, g * 2 + half] = bottom
+    for g in range(rows // 8):
+        edge = jnp.zeros((levs, cols), jnp.float32)
+        for i in range(8):
+            for f, ref in enumerate(fields):
+                x = ref[:, g * 8 + i, :]
+                main[g * 8 + i + 2, f] = x
+                base = 16 * i + 4 * f
+                edge = jnp.where(lane // 4 == base // 4, pltpu.roll(x, (base + 2) % cols, 1), edge)
         col_buf[g] = edge
-        return 0
-
-    lax.fori_loop(0, levs // 8, pack_edges, 0)
 
     for load in loads[3:]:
         load.wait()
@@ -197,14 +188,13 @@
         k = len(halo)
         halo.append(remote(src, dst, halo_send.at[k], halo_recv.at[k], dev))
 
-    edge_copy(row_buf.at[0], row_in.at[0], (up, py))
-    edge_copy(row_buf.at[1], row_in.at[1], (down, py))
+    edge_copy(main.at[pl.ds(2, 2)], main.at[pl.ds(rows + 2, 2)], (up, py))
+    edge_copy(main.at[pl.ds(rows, 2)], main.at[pl.ds(0, 2)], (down, py))
     edge_copy(col_buf, col_in.at[0], (px, left))
     edge_copy(col_buf, col_in.at[1], (px, right))
     for k, (step_x, step_y) in enumerate(CORNERS):
-        part = pl.ds(0, 8) if step_x < 0 else pl.ds(rows - 8, 8)
         edge_copy(
-            col_buf.at[:, part],
+            col_buf.at[0 if step_x < 0 else rows // 8 - 1],
             corner_in.at[k],
             (up if step_x < 0 else down, left if step_y < 0 else right),
         )
@@ -225,55 +215,52 @@
     for copy in halo:
         copy.wait()
 
-    def advance(g, _):
-        low = row8 < 4
-        from_left = jnp.concatenate(
-            [col_in[1, g // 2], jnp.where(low, corner_in[1, g // 2], corner_in[3, g // 2])], axis=0
-        )
-        from_right = jnp.concatenate(
-            [col_in[0, g // 2], jnp.where(low, corner_in[0, g // 2], corner_in[2, g // 2])], axis=0
-        )
-        sides = jnp.where(lane24 % 4 < 2, from_left, from_right)
-        sides = pltpu.roll(sides, 64 * (g % 2), 1)
-        for i in range(4):
-            lev = g * 4 + i
-            whole = []
-            for f, ref in enumerate(fields):
-                below = row_in[0, f, g]
-                above = row_in[1, f, g]
-                if i:
-                    below = pltpu.roll(below, 8 - 2 * i, 0)
-                if (6 - 2 * i) % 8:
-                    above = pltpu.roll(above, 6 - 2 * i, 0)
-                middle = jnp.concatenate([ref[lev], jnp.where(low, below, above)], axis=0)
-                base = 16 * i + 4 * f
-                edge = pltpu.roll(sides, (2 * cols - base - 2) % cols, 1)
-                whole.append(jnp.concatenate([middle, edge], axis=1))
-            u, v, t = whole
-            coef = hyper[lev]
-            rate = damp[lev]
-            div = diff_x(u) + diff_y(v)
-            u_in = u[:rows, :cols]
-            v_in = v[:rows, :cols]
-            t_in = t[:rows, :cols]
-            u_out[lev] = (
-                u_in
-                - coef * laplace(laplace(u))[:rows, :cols]
-                + rate * diff_x(div)[:rows, :cols]
-            )
-            v_out[lev] = (
-                v_in
-                - coef * laplace(laplace(v))[:rows, :cols]
-                + rate * diff_y(div)[:rows, :cols]
-            )
-            drift = u_in * diff_x(t)[:rows, :cols] + v_in * diff_y(t)[:rows, :cols]
-            t_out[lev] = t_in - coef * laplace(laplace(t))[:rows, :cols] - 0.5 * drift
-        return 0
-
-    lax.fori_loop(0, levs // 4, advance, 0)
+    from_left = lane % 4 < 2
+    edges = [jnp.where(from_left, corner_in[3], corner_in[2])]
+    for g in range(rows // 8):
+        edges.append(jnp.where(from_left, col_in[1, g], col_in[0, g]))
+    edges.append(jnp.where(from_left, corner_in[1], corner_in[0]))
+    for e in range(rows + 4):
+        at = (e + 6) % 8
+        for f in range(3):
+            side[e, f] = pltpu.roll(edges[(e + 6) // 8], (2 * cols - 16 * at - 4 * f - 2) % cols, 1)
+
+    def first(e, _):
+        def near(f, step):
+            return main[e + step, f], side[e + step, f]
+
+        for f in range(3):
+            lap = laplace(lane, near(f, -1), near(f, 0), near(f, 1))
+            lap_main[e, f] = lap[0]
+            lap_side[e, f] = lap[1]
+        below, above = near(0, 1), near(0, -1)
+        change = diff_y(lane, near(1, 0))
+        lap_main[e, 3] = (below[0] - above[0]) * 0.5 + change[0]
+        lap_side[e, 3] = (below[1] - above[1]) * 0.5 + change[1]
+        return 0
+
+    lax.fori_loop(1, rows + 3, first, 0)
 
     for r in range(rows):
-        line = t_out[:, r, :]
+        e = r + 2
+
+        def lap_near(f, step):
+            return lap_main[e + step, f], lap_side[e + step, f]
+
+        def second(f):
+            return laplace(lane, lap_near(f, -1), lap_near(f, 0), lap_near(f, 1))[0]
+
+        coef = coefs[0]
+        rate = coefs[1]
+        u, v, t = main[e, 0], main[e, 1], main[e, 2]
+        grad_x = (lap_main[e + 1, 3] - lap_main[e - 1, 3]) * 0.5
+        grad_y = diff_y(lane, lap_near(3, 0))[0]
+        theta_x = (main[e + 1, 2] - main[e - 1, 2]) * 0.5
+        theta_y = diff_y(lane, (t, side[e, 2]))[0]
+        u_out[:, r, :] = u - coef * second(0) + rate * grad_x
+        v_out[:, r, :] = v - coef * second(1) + rate * grad_y
+        line = t - coef * second(2) - 0.5 * (u * theta_x + v * theta_y)
+        t_out[:, r, :] = line
         for step in range(2):
             if step:
                 line = pltpu.roll(line, cols - 1, 1)
@@ -308,7 +295,7 @@
             hot = jnp.concatenate([hot, hot], axis=0)
             found = jnp.dot(table[...], hot, preferred_element_type=jnp.float32)
             zero = jnp.zeros((levs, width), jnp.float32)
-            base, nxt, side = zero, zero, zero
+            base, nxt, beside = zero, zero, zero
             before = None
             for r in range(rows):
                 at = r * 2 * levs
@@ -318,13 +305,13 @@
                 if r < rows - 1:
                     here = jnp.broadcast_to(row == r, (levs, width))
                     base = jnp.where(here, line, base)
-                    side = jnp.where(here, found[at + levs : at + 2 * levs], side)
+                    beside = jnp.where(here, found[at + levs : at + 2 * levs], beside)
                     before = here
             level = piece(src, 1, j).astype(jnp.int32)
             frac = piece(src, 2, j)
             w0 = piece(src, 3, j)
             w1 = piece(src, 4, j)
-            column = w0 * base + w1 * nxt + (1.0 - w0 - w1) * side
+            column = w0 * base + w1 * nxt + (1.0 - w0 - w1) * beside
             share = jnp.where(lev_iota == level, 1.0 - frac, 0.0)
             share = jnp.where(lev_iota == level + 1, frac, share)
             model = jnp.sum(column * share, axis=0, keepdims=True)
@@ -435,11 +422,14 @@
                 pltpu.VMEM((count, FIELDS, tiles, 128), f32),
                 pltpu.VMEM((count, tiles, 128), f32),
                 pltpu.VMEM((count, tiles, 128), f32),
-                pltpu.VMEM((2, 3, levs // 4, 8, cols), f32),
-                pltpu.VMEM((2, 3, levs // 4, 8, cols), f32),
-                pltpu.VMEM((levs // 8, rows, cols), f32),
-                pltpu.VMEM((2, levs // 8, rows, cols), f32),
-                pltpu.VMEM((4, levs // 8, 8, cols), f32),
+                pltpu.VMEM((2, levs, cols), f32),
+                pltpu.VMEM((rows + 4, 3, levs, cols), f32),
+                pltpu.VMEM((rows + 4, 3, levs, cols), f32),
+                pltpu.VMEM((rows + 4, 4, levs, cols), f32),
+                pltpu.VMEM((rows + 4, 4, levs, cols), f32),
+                pltpu.VMEM((rows // 8, levs, cols), f32),
+                pltpu.VMEM((2, rows // 8, levs, cols), f32),
+                pltpu.VMEM((4, levs, cols), f32),
                 pltpu.VMEM((rows * 2 * levs, 2 * cols), jnp.bfloat16),
                 pltpu.SemaphoreType.DMA((count,)),
                 pltpu.SemaphoreType.DMA((count,)),

time: 45.4 us -> 42.6 us (0.938)
  Pallas kernels: 44.6 us -> 41.8 us
    pallas_call x1, Pallas kernels: 42.5 us -> 39.8 us  [on_device(): pl.pallas_call(functools.partial(kernel, (n_px, n_py, tiles)), out_shape=...]
where the time goes in v6:
time: 42.6 us; the launch traced here: 42.5 us
  Pallas kernels  41.8 us (98%)
  between operations  0.64 us (2%)
    pallas_call x1, Pallas kernels, on_device(): pl.pallas_call(functools.partial(kernel, (n_px, n_py, tiles)), out_shape=...  39.8 us
    pallas_call x1, Pallas kernels, on_device(): pl.pallas_call(hand_over, out_shape=[jax.ShapeDtypeStruct(x.shape, x.dtyp...  2.03 us

profile of v6, /device:TPU:0, one launch (start us, length us, event | category | flops | bytes accessed | tf_op | source)
XLA Modules:
  0.0 42.5 jit_solution(12984848176862800571)
XLA Ops:
  0.6 39.8 %shard_map.138 = (f32[32,16,128]{2,1,0:T(8,128)}, f32[32,16,128]{2,1,0:T(8,128)}, f32[32,16,128]{2,1,0:T(8,128)}, f32[1,32,512]{2,1,0:T(8,128)}) custom-call(f32[32]{0:T(128)} %hyper.1, f32[32]{0:T(128)} %damp.1, f32[32,16,128]{2,1,0:T(8,128)} %u_hbm.1, f32[32,16,128]{2,1,0:T(8,128)} %v_hbm.1, f32[32,16,128]{2,1,0:T(8,128)} %t_hbm.1, ...), custom_call_target="tpu_custom_call" | custom-call | tf_op jit(solution)/shard_map/pallas_call | solution.py:406
  40.4 2.0 %shard_map.139 = (f32[32,16,128]{2,1,0:T(8,128)}, f32[32,16,128]{2,1,0:T(8,128)}, f32[32,16,128]{2,1,0:T(8,128)}, f32[1,32,512]{2,1,0:T(8,128)}) custom-call(f32[32,16,128]{2,1,0:T(8,128)} %get-tuple-element.12.refs_0_, f32[32,16,128]{2,1,0:T(8,128)} %get-tuple-element.13.refs_1_, f32[32,16,128]{2,1,0:T(8,128)} %get-tuple-element.14.refs_2_, ...), custom_call_target="tpu_custom_call" | custom-call | tf_op jit(solution)/shard_map/pallas_call | solution.py:456

commit v7 on v6

--- a/solution.py
+++ b/solution.py
@@ -288,12 +288,19 @@
                 out_buf.at[src], in_buf.at[src], obs_send.at[src], obs_recv.at[src], place(src)
             ).wait_recv()
 
+        cells = [piece(src, 0, j).astype(jnp.int32) for j in range(chunks)]
+        hot = jnp.concatenate(
+            [
+                jnp.where(col_iota == (cell & (cols - 1)), 1.0, 0.0).astype(jnp.bfloat16)
+                for cell in cells
+            ],
+            axis=1,
+        )
+        hot = jnp.concatenate([hot, hot], axis=0)
+        products = jnp.dot(table[...], hot, preferred_element_type=jnp.float32)
         for j in range(chunks):
-            cell = piece(src, 0, j).astype(jnp.int32)
-            row = cell // cols
-            hot = jnp.where(col_iota == (cell & (cols - 1)), 1.0, 0.0).astype(jnp.bfloat16)
-            hot = jnp.concatenate([hot, hot], axis=0)
-            found = jnp.dot(table[...], hot, preferred_element_type=jnp.float32)
+            row = cells[j] // cols
+            found = products[:, j * width : (j + 1) * width]
             zero = jnp.zeros((levs, width), jnp.float32)
             base, nxt, beside = zero, zero, zero
             before = None

time: 42.6 us -> 42.6 us (level)
  no operation moved by 1% of the time
where the time goes in v7:
time: 42.6 us; the launch traced here: 42.5 us
  Pallas kernels  41.8 us (98%)
  between operations  0.64 us (2%)
    pallas_call x1, Pallas kernels, on_device(): pl.pallas_call(functools.partial(kernel, (n_px, n_py, tiles)), out_shape=...  39.8 us
    pallas_call x1, Pallas kernels, on_device(): pl.pallas_call(hand_over, out_shape=[jax.ShapeDtypeStruct(x.shape, x.dtyp...  2.03 us

profile of v7, /device:TPU:0, one launch (start us, length us, event | category | flops | bytes accessed | tf_op | source)
XLA Modules:
  0.0 42.5 jit_solution(14989484416283873573)
XLA Ops:
  0.6 39.8 %shard_map.138 = (f32[32,16,128]{2,1,0:T(8,128)}, f32[32,16,128]{2,1,0:T(8,128)}, f32[32,16,128]{2,1,0:T(8,128)}, f32[1,32,512]{2,1,0:T(8,128)}) custom-call(f32[32]{0:T(128)} %hyper.1, f32[32]{0:T(128)} %damp.1, f32[32,16,128]{2,1,0:T(8,128)} %u_hbm.1, f32[32,16,128]{2,1,0:T(8,128)} %v_hbm.1, f32[32,16,128]{2,1,0:T(8,128)} %t_hbm.1, ...), custom_call_target="tpu_custom_call" | custom-call | tf_op jit(solution)/shard_map/pallas_call | solution.py:413
  40.4 2.0 %shard_map.139 = (f32[32,16,128]{2,1,0:T(8,128)}, f32[32,16,128]{2,1,0:T(8,128)}, f32[32,16,128]{2,1,0:T(8,128)}, f32[1,32,512]{2,1,0:T(8,128)}) custom-call(f32[32,16,128]{2,1,0:T(8,128)} %get-tuple-element.12.refs_0_, f32[32,16,128]{2,1,0:T(8,128)} %get-tuple-element.13.refs_1_, f32[32,16,128]{2,1,0:T(8,128)} %get-tuple-element.14.refs_2_, ...), custom_call_target="tpu_custom_call" | custom-call | tf_op jit(solution)/shard_map/pallas_call | solution.py:463
